TPU v7x, 768 devices: a whole 4x8x12 slice. The times are simulated.
768 devices in a mesh: mem: 96 (over z, x, core), grp: 8 (over y).
Axes of the slice: x: 4, y: 8, z: 12, core: 2. Of those that a mesh axis runs over, the one named last changes fastest.
Arguments:
- state: float32 [1024, 768, 128], P('grp', 'mem'), may hold values from -6 to 6
- obs_ens: float32 [1024, 768, 128], P('grp', 'mem'), may hold values from -6 to 6
- obs_value: float32 [768, 128], P(('mem', 'grp')), may hold values from -8 to 8
- obs_precision: float32 [768, 128], P(('mem', 'grp')), may hold values from 0.5 to 4
- locality: int32 [768, 384], P(('mem', 'grp')), may hold values from 0 to 383, as said below
- obs_count: int32 [768], P(('mem', 'grp')), may hold values from 48 to 384, as said below
- land_mask: int32 [768, 128], P(('mem', 'grp')), may hold values 0 or 1
Outputs:
- analysis: float32 [1024, 768, 128], P(None, ('mem', 'grp'))
Inputs may be any that keep to these rules, and one draw needn't show every extreme that they name: `locality`: pool indices 0 to 127 name the previous patch's observations, 128 to 255 the patch's own, the rest the next patch's; every row lists each pool index once. `obs_count`: some patch has all 384 rows live.
All inputs are finite; a program needn't handle non-finite values. No bound on the sum of `land_mask` on one device may be relied on, other than what follows from the above.
Results may differ from a plain program's by a relative error of at most 0.0003.
Values sent between devices are 32-bit elements; how exact they have to be, the bound alone decides.
No kernel may reach another device: no remote copies, remote signals or barrier semaphores. Data moves between devices by JAX's collectives and lax.ppermute only.
A program may use at most 64 MiB of HBM per device.

v0:
```python
import math

import jax
import jax.numpy as jnp
from jax import lax
from jax.sharding import PartitionSpec as P

highest = lax.Precision.HIGHEST


def with_halo(cells, sides, width):
    for axis, dim in sides:
        count = lax.axis_size(axis)
        head = lax.slice_in_dim(cells, 0, width, axis=dim)
        tail = lax.slice_in_dim(cells, cells.shape[dim] - width, cells.shape[dim], axis=dim)
        cells = jnp.concatenate(
            [
                lax.ppermute(tail, axis, [(i, (i + 1) % count) for i in range(count)]),
                cells,
                lax.ppermute(head, axis, [((i + 1) % count, i) for i in range(count)]),
            ],
            axis=dim,
        )
    return cells


def finish(background, centred, weights, depart, gram_matrix, land_row):
    members = background.shape[0]
    system = gram_matrix + (members - 1) * jnp.eye(members, dtype=jnp.float32)
    factor = jnp.linalg.cholesky(system)
    forcing = jnp.dot(centred, weights * depart, precision=highest)[:, None]
    halfway = jax.scipy.linalg.solve_triangular(factor, forcing, lower=True)
    mean_weights = jax.scipy.linalg.solve_triangular(factor, halfway, lower=True, trans=1)[:, 0]
    state_mean = jnp.mean(background, axis=0)
    deviate = background - state_mean
    spread = math.sqrt(members - 1) * jax.scipy.linalg.solve_triangular(factor, deviate, lower=True)
    increment = jnp.dot(mean_weights, deviate, precision=highest)
    analysed = state_mean + increment + spread
    return jnp.where(land_row > 0, analysed, background)


def prepare(pooled, values, precise, picks, live_count):
    chosen = jnp.take(pooled, picks, axis=1)
    obs_mean = jnp.mean(chosen, axis=0)
    centred = chosen - obs_mean
    live = jnp.arange(picks.shape[0], dtype=jnp.int32) < live_count
    weights = jnp.where(live, jnp.take(precise, picks), jnp.float32(0.0))
    depart = jnp.take(values, picks) - obs_mean
    return (centred, weights, depart)


def local(state, obs_ens, obs_value, obs_precision, locality, obs_count, land_mask):
    owned = obs_ens.shape[2]
    info = jnp.stack([obs_value, obs_precision], axis=0)
    whole_state, whole_obs = (
        lax.all_to_all(state, "grp", split_axis=1, concat_axis=0, tiled=True),
        lax.all_to_all(obs_ens, "grp", split_axis=1, concat_axis=0, tiled=True),
    )
    members = whole_state.shape[0]
    joined = jnp.concatenate([whole_obs, info], axis=0)
    extended = with_halo(joined, ((("mem", "grp"), 1),), 1)
    ext_obs = extended[:members]
    ext_info = extended[members:]
    pooled = ext_obs.reshape(members, 3 * owned)
    values = ext_info[0, 0:3, :].reshape(-1)
    precise = ext_info[1, 0:3, :].reshape(-1)
    live_count = obs_count[0]
    centred, weights, depart = prepare(pooled, values, precise, locality[0], live_count)
    gram_matrix = lax.dot_general(
        centred * weights, centred, (((1,), (1,)), ((), ())), precision=highest
    )
    results = [finish(whole_state[:, 0, :], centred, weights, depart, gram_matrix, land_mask[0])]
    return jnp.stack(results, axis=1)


def solution(mesh):
    placed = (
        P("grp", "mem", None),
        P("grp", "mem", None),
        P(("mem", "grp"), None),
        P(("mem", "grp"), None),
        P(("mem", "grp"), None),
        P(("mem", "grp")),
        P(("mem", "grp"), None),
    )
    return jax.shard_map(
        local, mesh=mesh, in_specs=placed, out_specs=P(None, ("mem", "grp"), None), check_vma=False
    )
```

profile of v0, /device:TPU:577, one launch (start us, length us, event | category | flops | bytes accessed | tf_op | source)
XLA Modules:
  0.0 427.2 jit_solution(7552692774666144356)
XLA Ops:
  0.0 2.0 copy.21
  2.0 6.8 %all-to-all-start.1 = ((f32[128,8,128]{2,0,1:T(8,128)}), f32[128,8,128]{2,0,1:T(8,128)S(1)}, u32[]{:S(2)}, u32[]{:S(2)}) async-start(f32[128,8,128]{2,0,1:T(8,128)} %copy.21), calls=%async_computation.1 | async-start | bytes 1048576 | tf_op jit(solution)/shard_map/all_to_all | solution.py:57
  8.8 1.9 copy.20
  10.8 16.0 %all-to-all-done.1 = f32[128,8,128]{2,0,1:T(8,128)S(1)} async-done(((f32[128,8,128]{2,0,1:T(8,128)}), f32[128,8,128]{2,0,1:T(8,128)S(1)}, u32[]{:S(2)}, u32[]{:S(2)}) %all-to-all-start.1) | async-done | bytes 524320 | tf_op jit(solution)/shard_map/all_to_all | solution.py:57
  26.8 3.5 all-to-all-start
  31.2 3.3 copy.24
  34.5 3.3 collective-permute-start
  37.8 3.8 collective-permute-start.1
  41.6 6.5 %all-to-all-done = f32[128,8,128]{2,0,1:T(8,128)S(1)} async-done(((f32[128,8,128]{2,0,1:T(8,128)}), f32[128,8,128]{2,0,1:T(8,128)S(1)}, u32[]{:S(2)}, u32[]{:S(2)}) %all-to-all-start) | async-done | bytes 524320 | tf_op jit(solution)/shard_map/all_to_all | solution.py:56
  50.0 6.5 %collective-permute-done = f32[1026,1,128]{2,1,0:T(1,128)S(1)} collective-permute-done((f32[1026,1,128]{2,1,0:T(1,128)S(1)}, f32[1026,1,128]{2,1,0:T(1,128)S(1)}, u32[]{:S(2)}, u32[]{:S(2)}) %collective-permute-start) | collective-permute-done | bytes 525344 | tf_op jit(solution)/shard_map/ppermute | solution.py:18
  56.8 1.3 slice.424
  58.1 1.9 copy.28
  60.0 2.8 gather_fusion.1
  62.8 2.8 gather_fusion.2
  65.6 1.8 gather_fusion
  67.7 9.1 %fusion.4 = f32[1024,1024]{1,0:T(8,128)} fusion(f32[384,1024]{1,0:T(8,128)S(1)} %gather_fusion, f32[384]{0:T(512)S(1)} %get-tuple-element.67, f32[384]{0:T(512)S(1)} %get-tuple-element.25, pred[384]{0:T(512)(128)(4,1)S(1)} %compare_and_fusion), kind=kOutput, calls=%fused_computation.16 | convolution fusion | flops 4833804288 | bytes 5770624 | tf_op jit(solution)/shard_map/dot_general | solution.py:69
  76.7 5.8 %copy.29 = f32[1024,1024]{0,1:T(8,128)} copy(f32[1024,1024]{1,0:T(8,128)} %fusion.4) | data formatting | bytes 8388608 | tf_op jit(solution)/shard_map/dot_general | solution.py:69
  82.5 4.4 %fusion.1 = f32[1024,1024]{1,0:T(8,128)S(1)} fusion(f32[1024,1024]{0,1:T(8,128)} %copy.29, f32[1024,1024]{1,0:T(8,128)} %fusion.4), kind=kLoop, calls=%fused_computation.8 | loop fusion | flops 8388608 | bytes 12582912 | tf_op jit(solution)/shard_map/jit(cholesky)/div | solution.py:30
  87.0 1.9 copy-done.3
  88.9 11.7 %cholesky.222 = f32[128,128]{1,0:T(8,128)S(1)} custom-call(f32[128,128]{1,0:T(8,128)S(1)} %cholesky.577), custom_call_target="Cholesky" | custom-call | tf_op jit(solution)/shard_map/jit(cholesky)/cholesky | solution.py:30
  100.7 2.5 cholesky.254
  103.2 9.8 %custom-call.69 = f32[1,128,128]{1,2,0:T(8,128)S(1)} custom-call(f32[1,128,128]{2,1,0:T(8,128)S(1)} %get-tuple-element.66), custom_call_target="InvertDiagBlocksLowerTriangular" | custom-call | tf_op jit(solution)/shard_map/jit(cholesky)/cholesky | solution.py:30
  113.0 2.4 constant_dynamic-update-slice_fusion.74
  115.3 1.5 convolution_subtract_fusion
  116.9 11.9 %cholesky.243 = f32[128,128]{1,0:T(8,128)S(1)} custom-call(f32[128,128]{1,0:T(8,128)S(1)} %cholesky.581), custom_call_target="Cholesky" | custom-call | tf_op jit(solution)/shard_map/jit(cholesky)/cholesky | solution.py:30
  130.8 9.8 %custom-call.70 = f32[1,128,128]{1,2,0:T(8,128)S(1)} custom-call(f32[1,128,128]{2,1,0:T(8,128)S(1)} %get-tuple-element.63), custom_call_target="InvertDiagBlocksLowerTriangular" | custom-call | tf_op jit(solution)/shard_map/jit(cholesky)/cholesky | solution.py:30
  140.6 1.2 convolution_dynamic-update-slice_fusion
  141.8 2.1 convolution_subtract_fusion.1
  143.9 11.7 %cholesky.466 = f32[128,128]{1,0:T(8,128)S(1)} custom-call(f32[128,128]{1,0:T(8,128)S(1)} %cholesky.586), custom_call_target="Cholesky" | custom-call | tf_op jit(solution)/shard_map/jit(cholesky)/cholesky | solution.py:30
  156.9 9.8 %custom-call.71 = f32[1,128,128]{1,2,0:T(8,128)S(1)} custom-call(f32[1,128,128]{2,1,0:T(8,128)S(1)} %get-tuple-element.60), custom_call_target="InvertDiagBlocksLowerTriangular" | custom-call | tf_op jit(solution)/shard_map/jit(cholesky)/cholesky | solution.py:30
  166.7 1.2 convolution_dynamic-update-slice_fusion.1
  167.9 2.3 convolution_subtract_fusion.2
  170.3 11.9 %cholesky.485 = f32[128,128]{1,0:T(8,128)S(1)} custom-call(f32[128,128]{1,0:T(8,128)S(1)} %cholesky.591), custom_call_target="Cholesky" | custom-call | tf_op jit(solution)/shard_map/jit(cholesky)/cholesky | solution.py:30
  183.5 9.8 %custom-call.72 = f32[1,128,128]{1,2,0:T(8,128)S(1)} custom-call(f32[1,128,128]{2,1,0:T(8,128)S(1)} %get-tuple-element.57), custom_call_target="InvertDiagBlocksLowerTriangular" | custom-call | tf_op jit(solution)/shard_map/jit(cholesky)/cholesky | solution.py:30
  193.3 1.1 convolution_dynamic-update-slice_fusion.2
  194.4 2.3 convolution_subtract_fusion.3
  196.8 11.7 %cholesky.504 = f32[128,128]{1,0:T(8,128)S(1)} custom-call(f32[128,128]{1,0:T(8,128)S(1)} %cholesky.596), custom_call_target="Cholesky" | custom-call | tf_op jit(solution)/shard_map/jit(cholesky)/cholesky | solution.py:30
  209.9 10.2 %custom-call.73 = f32[1,128,128]{1,2,0:T(8,128)S(1)} custom-call(f32[1,128,128]{2,1,0:T(8,128)S(1)} %get-tuple-element.54), custom_call_target="InvertDiagBlocksLowerTriangular" | custom-call | tf_op jit(solution)/shard_map/jit(cholesky)/cholesky | solution.py:30
  221.1 2.3 convolution_subtract_fusion.4
  223.4 11.7 %cholesky.524 = f32[128,128]{1,0:T(8,128)S(1)} custom-call(f32[128,128]{1,0:T(8,128)S(1)} %cholesky.601), custom_call_target="Cholesky" | custom-call | tf_op jit(solution)/shard_map/jit(cholesky)/cholesky | solution.py:30
  236.4 9.8 %custom-call.74 = f32[1,128,128]{1,2,0:T(8,128)S(1)} custom-call(f32[1,128,128]{2,1,0:T(8,128)S(1)} %get-tuple-element.51), custom_call_target="InvertDiagBlocksLowerTriangular" | custom-call | tf_op jit(solution)/shard_map/jit(cholesky)/cholesky | solution.py:30
  247.1 2.0 convolution_subtract_fusion.5
  249.2 11.8 %cholesky.544 = f32[128,128]{1,0:T(8,128)S(1)} custom-call(f32[128,128]{1,0:T(8,128)S(1)} %cholesky.606), custom_call_target="Cholesky" | custom-call | tf_op jit(solution)/shard_map/jit(cholesky)/cholesky | solution.py:30
  262.3 9.8 %custom-call.75 = f32[1,128,128]{1,2,0:T(8,128)S(1)} custom-call(f32[1,128,128]{2,1,0:T(8,128)S(1)} %get-tuple-element.48), custom_call_target="InvertDiagBlocksLowerTriangular" | custom-call | tf_op jit(solution)/shard_map/jit(cholesky)/cholesky | solution.py:30
  273.0 1.8 convolution_subtract_fusion.11
  274.7 11.7 %cholesky.562 = f32[128,128]{1,0:T(8,128)S(1)} custom-call(f32[128,128]{1,0:T(8,128)S(1)} %convolution_subtract_fusion.11), custom_call_target="Cholesky" | custom-call | tf_op jit(solution)/shard_map/jit(cholesky)/cholesky | solution.py:30
  292.8 4.8 %select_select_fusion = f32[1024,1024]{1,0:T(8,128)} fusion(f32[1024,1024]{1,0:T(8,128)} %get-tuple-element.46, pred[]{:T(512)S(6)} %cholesky.576), kind=kLoop, calls=%fused_computation.5 | loop fusion | flops 4194304 | bytes 8388609 | tf_op jit(solution)/shard_map/jit(_solve_triangular)/triangular_solve | solution.py:33
  297.7 27.6 %while.1 = (s32[]{:T(128)}, f32[1024,1024]{1,0:T(8,128)}, s32[8,2]{0,1:T(2,128)S(1)}, f32[8,128,128]{2,1,0:T(8,128)}, s32[]{:T(128)}) while((s32[]{:T(128)}, f32[1024,1024]{1,0:T(8,128)}, s32[8,2]{0,1:T(2,128)S(1)}, f32[8,128,128]{2,1,0:T(8,128)}, s32[]{:T(128)}) %tuple.78), condition=%wide.while_cond, body=%wide.while_body.sunk | while | flops 2 | bytes 132705 | solution.py:33
  298.3 2.8 bitcast_dynamic-update-slice_fusion.2
  301.8 2.8 bitcast_dynamic-update-slice_fusion.2
  305.2 2.8 bitcast_dynamic-update-slice_fusion.2
  308.7 2.8 bitcast_dynamic-update-slice_fusion.2
  312.2 2.9 bitcast_dynamic-update-slice_fusion.2
  315.6 2.8 bitcast_dynamic-update-slice_fusion.2
  319.1 2.8 bitcast_dynamic-update-slice_fusion.2
  322.6 2.8 bitcast_dynamic-update-slice_fusion.2
  325.3 79.6 %custom-call.76 = f32[8,128,128]{1,2,0:T(8,128)S(1)} custom-call(f32[8,128,128]{2,1,0:T(8,128)} %get-tuple-element.13), custom_call_target="InvertDiagBlocksLowerTriangular" | custom-call | tf_op jit(solution)/shard_map/jit(_solve_triangular)/triangular_solve | solution.py:33
  405.3 1.2 convolution_subtract_fusion.10
  406.5 1.1 fusion.2
  409.0 1.1 fusion.19
  410.3 1.2 fusion.39
  411.8 1.2 fusion.24
  413.2 1.4 fusion.37
  414.8 1.4 fusion.26
  (153 shorter events, 33.5 us)
Async XLA Ops:
  0.0 30.9 %copy-start.6 = (s32[1,384]{1,0:T(1,128)S(1)}, s32[1,384]{1,0:T(1,128)}, u32[]{:S(2)}) copy-start(s32[1,384]{1,0:T(1,128)} %param.13) | copy-start | bytes 4612
  0.0 31.0 %copy-start.9 = (s32[1,128]{1,0:T(1,128)S(1)}, s32[1,128]{1,0:T(1,128)}, u32[]{:S(2)}) copy-start(s32[1,128]{1,0:T(1,128)} %param.15) | copy-start | bytes 1540
  0.0 31.1 %copy-start.7 = (f32[1,128]{1,0:T(1,128)S(1)}, f32[1,128]{1,0:T(1,128)}, u32[]{:S(2)}) copy-start(f32[1,128]{1,0:T(1,128)} %param.11) | copy-start | bytes 1540
  0.0 31.1 %copy-start.8 = (f32[1,128]{1,0:T(1,128)S(1)}, f32[1,128]{1,0:T(1,128)}, u32[]{:S(2)}) copy-start(f32[1,128]{1,0:T(1,128)} %param.12) | copy-start | bytes 1540
  2.0 24.8 %all-to-all-start.1 = ((f32[128,8,128]{2,0,1:T(8,128)}), f32[128,8,128]{2,0,1:T(8,128)S(1)}, u32[]{:S(2)}, u32[]{:S(2)}) async-start(f32[128,8,128]{2,0,1:T(8,128)} %copy.21), calls=%async_computation.1 | async-start | bytes 1048576 | tf_op jit(solution)/shard_map/all_to_all | solution.py:57
  26.8 21.4 %all-to-all-start = ((f32[128,8,128]{2,0,1:T(8,128)}), f32[128,8,128]{2,0,1:T(8,128)S(1)}, u32[]{:S(2)}, u32[]{:S(2)}) async-start(f32[128,8,128]{2,0,1:T(8,128)} %copy.20), calls=%async_computation | async-start | bytes 1048576 | tf_op jit(solution)/shard_map/all_to_all | solution.py:56
  34.5 22.0 %collective-permute-start = (f32[1026,1,128]{2,1,0:T(1,128)S(1)}, f32[1026,1,128]{2,1,0:T(1,128)S(1)}, u32[]{:S(2)}, u32[]{:S(2)}) collective-permute-start(f32[1026,1,128]{2,1,0:T(1,128)S(1)} %copy.24), channel_id=1, source_target_pairs={{0,1},{1,2},{2,3},{3,4},{4,5},{5,6},{6,7},{7,8},{8,9},{9,10},{10,1... | collective-permute-start | bytes 1575944 | tf_op jit(solution)/shard_map/ppermute | solution.py:18
  37.8 18.8 %collective-permute-start.1 = (f32[1026,1,128]{2,1,0:T(1,128)S(1)}, f32[1026,1,128]{2,1,0:T(1,128)S(1)}, u32[]{:S(2)}, u32[]{:S(2)}) collective-permute-start(f32[1026,1,128]{2,1,0:T(1,128)S(1)} %copy.24), channel_id=1, source_target_pairs={{1,0},{2,1},{3,2},{4,3},{5,4},{6,5},{7,6},{8,7},{9,8},{10,9},{11,1... | collective-permute-start | bytes 1575944 | tf_op jit(solution)/shard_map/ppermute | solution.py:20
  48.1 8.5 %copy-start.1 = (f32[128,8,128]{2,0,1:T(8,128)}, f32[128,8,128]{2,0,1:T(8,128)S(1)}, u32[]{:S(2)}) copy-start(f32[128,8,128]{2,0,1:T(8,128)S(1)} %all-to-all-done) | copy-start | bytes 1572868
  87.0 1.9 copy-start.3
  292.8 112.1 %copy-start.5 = (f32[1024,128]{1,0:T(8,128)S(1)}, f32[1024,128]{1,0:T(8,128)}, u32[]{:S(2)}) copy-start(f32[1024,128]{1,0:T(8,128)} %bitcast_subtract_fusion) | copy-start | bytes 1572868
  405.0 11.4 %copy-start = (f32[1024,1024]{1,0:T(8,128)S(1)}, f32[1024,1024]{1,0:T(8,128)}, u32[]{:S(2)}) copy-start(f32[1024,1024]{1,0:T(8,128)} %get-tuple-element.161) | copy-start | bytes 12582916
  419.6 5.8 %copy-start.4 = (f32[8,128,1,128]{3,1,0,2:T(8,128)S(1)}, f32[8,128,1,128]{3,1,0,2:T(8,128)}, u32[]{:S(2)}) copy-start(f32[8,128,1,128]{3,1,0,2:T(8,128)} %bitcast_subtract_fusion.1) | copy-start | bytes 1572868
  420.3 5.8 %copy-start.2 = (f32[128,8,128]{2,0,1:T(8,128)S(1)}, f32[128,8,128]{2,0,1:T(8,128)}, u32[]{:S(2)}) copy-start(f32[128,8,128]{2,0,1:T(8,128)} %copy-done.1) | copy-start | bytes 1572868
where the time goes:
time: 435 us; the launch traced here: 427 us
  other arithmetic  265 us (61%)
  local copies, waits for them, and re-layouts  56.3 us (13%)
  matrix products  52.6 us (12%)
  waiting for transfers between devices  29 us (7%)
  starting transfers between devices  17.4 us (4%)
  between operations  6.6 us (2%)
    another operation x31, other arithmetic, finish(): factor = jnp.linalg.cholesky(system)  173 us
    another operation x3, other arithmetic, finish(): jax.scipy.linalg.solve_triangular(factor, halfway, lower=True, trans=1)  84.5 us
    another operation x24, local copies, waits for them, and re-layouts  27.6 us
    another operation x14, matrix products, finish(): factor = jnp.linalg.cholesky(system)  23.1 us
    all_to_all x1, waiting for transfers between devices, local(): lax.all_to_all(obs_ens, 'grp', split_axis=1, concat_axis=0, tiled=True)  16 us
    another operation x15, matrix products, finish(): halfway = jax.scipy.linalg.solve_triangular(factor, forcing, lower=True)  9.46 us
    dot_general x1, matrix products, local(): lax.dot_general(centred * weights, centred, (((1,), (1,)), ((), ())), pre...  9.05 us
  transfers between devices with their start and end apart: 4, of which 3 were waited for; matrix products, arithmetic and copies ran while one was open for 2% of the time, Pallas kernels for 0%

commit v1 on v0

v1 whole, which is shorter than its diff:
```python
import jax
import jax.numpy as jnp
from jax import lax
from jax.experimental import pallas as pl
from jax.experimental.pallas import tpu as pltpu
from jax.sharding import PartitionSpec as P

CHAINS = 8
SUB = 16
CUT = 5
BLOCK = 128


def lane(x, i):
    return jnp.broadcast_to(x[:, i:i + 1], x.shape)


def split(x):
    hi = x.astype(jnp.bfloat16)
    rest = x - hi.astype(jnp.float32)
    mid = rest.astype(jnp.bfloat16)
    lo = (rest - mid.astype(jnp.float32)).astype(jnp.bfloat16)
    return hi, mid, lo


def left(x, axis):
    hi, mid, lo = split(x)
    return jnp.concatenate([hi, hi, mid, hi, lo, mid], axis=axis)


def right(x, axis):
    hi, mid, lo = split(x)
    return jnp.concatenate([hi, mid, hi, lo, hi, mid], axis=axis)


def dot(a, b, ca, cb):
    return lax.dot_general(a, b, (((ca,), (cb,)), ((), ())), preferred_element_type=jnp.float32)


def mm_nn(a, b):
    return dot(left(a, 1), right(b, 0), 1, 0)


def mm_nt(a, b):
    return dot(left(a, 1), right(b, 1), 1, 1)


def mm_tn(a, b):
    return dot(left(a, 0), right(b, 0), 0, 0)


def sub_block(mat, inv, wrow, q):
    iota = lax.broadcasted_iota(jnp.int32, (CHAINS, BLOCK), 1)
    base = q * SUB
    panels = SUB // 8

    def block(rows, first):
        return {(a, b): lane(rows[a], first + b) for a in range(8) for b in range(a, 8)}

    groups = [
        [mat[pl.ds(base + 8 * r + a, CHAINS, stride=BLOCK), :] for a in range(8)]
        for r in range(panels)
    ]
    coef = block(groups[0], base)
    for p in range(panels):
        first = base + 8 * p
        inside = (iota >= first) & (iota < first + 8)
        rows = [jnp.where(inside, jnp.where(iota == first + a, 1.0, 0.0), groups[p][a]) for a in range(8)]
        for r in range(p + 1, panels):
            groups[r] = [jnp.where(inside, 0.0, x) for x in groups[r]]
        done = []
        ahead = None
        for t in range(8):
            scale = lax.rsqrt(coef[t, t])
            w = rows[t] * scale
            done.append(w)
            inv[pl.ds(first + t, CHAINS, stride=BLOCK), :] = jnp.where(iota <= first + t, w, 0.0)
            wrow[pl.ds(8 * p + t, CHAINS, stride=SUB), :] = w
            m = {a: coef[t, a] * scale for a in range(t + 1, 8)}
            for a in range(t + 1, 8):
                for b in range(a, 8):
                    coef[a, b] = coef[a, b] - m[a] * m[b]
                rows[a] = rows[a] - m[a] * w
            if p + 1 < panels:
                if t == CUT:
                    ahead = block(groups[p + 1], first + 8)
                c = [lane(w, first + 8 + a) for a in range(8)]
                for a in range(8):
                    groups[p + 1][a] = groups[p + 1][a] - c[a] * w
                if t >= CUT:
                    for a in range(8):
                        for b in range(a, 8):
                            ahead[a, b] = ahead[a, b] - c[a] * c[b]
        if p + 1 < panels:
            coef = ahead
            for r in range(p + 2, panels):
                for a in range(8):
                    x = groups[r][a]
                    for t in range(8):
                        x = x - lane(done[t], base + 8 * r + a) * done[t]
                    groups[r][a] = x


def join(mat, wrow, q):
    base = q * SUB
    lanes = lax.broadcasted_iota(jnp.int32, (SUB, BLOCK), 1)
    drop = (lanes > lax.broadcasted_iota(jnp.int32, (SUB, BLOCK), 0) + base) & (lanes < base + SUB)
    below = BLOCK - base - SUB
    over = lax.broadcasted_iota(jnp.int32, (below, BLOCK), 1)
    clear = (over >= base) & (over < base + SUB)
    for c in range(CHAINS):
        w = wrow[c * SUB:(c + 1) * SUB, :]
        out = dot(left(w, 0), right(jnp.where(drop, 0.0, w), 0), 0, 0)
        at = pl.ds(c * BLOCK + base + SUB, below)
        mat[at, :] = jnp.where(clear, 0.0, mat[at, :]) - out[base + SUB:, :]


def inverse_factors(mat, inv, wrow):
    for q in range(BLOCK // SUB):
        sub_block(mat, inv, wrow, q)
        if (q + 1) * SUB < BLOCK:
            join(mat, wrow, q)


def at(k):
    return pl.ds(pl.multiple_of(k * BLOCK, BLOCK), BLOCK)


def analyse(members, own, before, after, state, value, precise, land, out, p00, p10, p11, p20, p21, p22,
            f, u, r, s, inv, wrow):
    blocks = members // BLOCK
    eye = (lax.broadcasted_iota(jnp.int32, (BLOCK, BLOCK), 0)
           == lax.broadcasted_iota(jnp.int32, (BLOCK, BLOCK), 1)).astype(jnp.float32)
    first_row = lax.broadcasted_iota(jnp.int32, (BLOCK, BLOCK), 0) == 0
    state_mean = jnp.mean(state[...], axis=0, keepdims=True)
    r[0:members, :] = state[...] - state_mean
    r[members:, :] = jnp.zeros((BLOCK, BLOCK), jnp.float32)
    for i, obs in enumerate((own, before, after)):
        scale = jnp.sqrt(precise[i:i + 1, :] * (1.0 / (members - 1)))
        mean = jnp.mean(obs[...], axis=0, keepdims=True)
        u[i, 0:members, :] = (obs[...] - mean) * scale
        u[i, members:, :] = jnp.where(first_row, (value[i:i + 1, :] - mean) * scale, 0.0)

    def gather(k, total):
        uk = [u[i, at(k), :] for i in range(3)]
        cols = right(jnp.concatenate([r[at(k), :]] + uk, axis=1), 0)
        rows = [left(x, 0) for x in uk]
        g0 = dot(rows[0], cols[:, :2 * BLOCK], 0, 0)
        g1 = dot(rows[1], cols[:, :3 * BLOCK], 0, 0)
        g2 = dot(rows[2], cols, 0, 0)
        new = [g0[:, :BLOCK], g1[:, :BLOCK], g2[:, :BLOCK], g0[:, BLOCK:], g1[:, BLOCK:2 * BLOCK], g1[:, 2 * BLOCK:],
               g2[:, BLOCK:2 * BLOCK], g2[:, 2 * BLOCK:3 * BLOCK], g2[:, 3 * BLOCK:]]
        dest = [f.at[0], f.at[1], f.at[2], p00, p10, p11, p20, p21, p22]
        prev = at(jnp.maximum(k - 1, 0))
        starts = [0.0, 0.0, 0.0, eye, 0.0, eye, 0.0, 0.0, eye]
        for ref, x, start in zip(dest, new, starts):
            ref[at(k), :] = x + jnp.where(k == 0, start, ref[prev, :])
        s[at(k + 1), :] = eye
        return total

    lax.fori_loop(0, blocks, gather, 0)
    s[at(0), :] = eye + sum(mm_nt(u[i, at(0), :], u[i, at(0), :]) for i in range(3))

    def stage(i, c):
        k = c + 1
        t = inv[at(c), :]
        lower = ([p10, p20], [p21], [])[i]
        parts = [ref[at(c), :] for ref in lower] + [u[i, at(k), :]]
        rows = mm_nt(jnp.concatenate(parts, axis=0), t)
        top = (2 - i) * BLOCK
        g = mm_nn(t, f[i, at(c), :])
        y = rows[top:, :]
        s[at(k), :] += mm_nt(y, y)
        change = mm_nn(rows, g)
        r[at(k), :] -= change[top:, :]
        for n in range(2 - i):
            f[i + 1 + n, at(c), :] -= change[n * BLOCK:(n + 1) * BLOCK, :]
        if top:
            upd = mm_nt(rows, rows[:top, :])
            u[i + 1, at(k), :] -= upd[top:, :BLOCK]
            if i == 0:
                p11[at(c), :] -= upd[:BLOCK, :BLOCK]
                p21[at(c), :] -= upd[BLOCK:top, :BLOCK]
                p22[at(c), :] -= upd[BLOCK:top, BLOCK:]
                u[2, at(k), :] -= upd[top:, BLOCK:]
            else:
                p22[at(c), :] -= upd[:BLOCK, :BLOCK]

    for i, diag in enumerate((p00, p11, p22)):
        inverse_factors(diag, inv, wrow)

        def body(c, carry, i=i):
            stage(i, c)
            return carry

        lax.fori_loop(0, CHAINS, body, 0)
    inverse_factors(s, inv, wrow)
    increment = -r[members:members + 1, :]
    wet = land[0:1, :] > 0

    def final(k, carry):
        spread = mm_nn(inv[at(k), :], r[at(k), :])
        out[at(k), :] = jnp.where(wet, state_mean + increment + spread, state[at(k), :])
        return carry

    lax.fori_loop(0, blocks, final, 0)


def compute(own, before, after, state, value, precise, land):
    members = own.shape[0]
    big = pltpu.VMEM((members, BLOCK), jnp.float32)
    return pl.pallas_call(
        lambda *refs: analyse(members, *refs),
        out_shape=jax.ShapeDtypeStruct((members, BLOCK), jnp.float32),
        scratch_shapes=[big] * 6 + [
            pltpu.VMEM((3, members, BLOCK), jnp.float32),
            pltpu.VMEM((3, members + BLOCK, BLOCK), jnp.float32),
            pltpu.VMEM((members + BLOCK, BLOCK), jnp.float32),
            pltpu.VMEM((members + BLOCK, BLOCK), jnp.float32),
            big,
            pltpu.VMEM((CHAINS * SUB, BLOCK), jnp.float32),
        ],
        compiler_params=pltpu.CompilerParams(vmem_limit_bytes=48 * 1024 * 1024),
    )(own, before, after, state, value, precise, land)


def ring(x, step):
    count = lax.axis_size(("mem", "grp"))
    return lax.ppermute(x, ("mem", "grp"), [(i, (i + step) % count) for i in range(count)])


def local(state, obs_ens, obs_value, obs_precision, locality, obs_count, land_mask):
    info = jnp.concatenate([obs_value, obs_precision], axis=0)
    info = jnp.stack([info, ring(info, 1), ring(info, -1)], axis=0)
    spots = jnp.roll(jnp.arange(3 * BLOCK, dtype=jnp.int32), -BLOCK).reshape(3, BLOCK)
    spots = jnp.stack([spots[0], spots[2], spots[1]], axis=0)
    rank = jnp.arange(locality.shape[1], dtype=jnp.int32)
    live = jnp.where(rank < obs_count[0], locality[0], -1)
    live = jnp.any(spots[:, None, :] == live[None, :, None], axis=1)
    value, precise = info[:, 0, :], jnp.where(live, info[:, 1, :], 0.0)
    whole_obs = lax.all_to_all(obs_ens, "grp", split_axis=1, concat_axis=0, tiled=True)[:, 0, :]
    whole_state = lax.all_to_all(state, "grp", split_axis=1, concat_axis=0, tiled=True)[:, 0, :]
    before, after = ring(whole_obs, 1), ring(whole_obs, -1)
    out = compute(whole_obs, before, after, whole_state, value, precise, land_mask)
    return out[:, None, :]


def solution(mesh):
    placed = (
        P("grp", "mem", None),
        P("grp", "mem", None),
        P(("mem", "grp"), None),
        P(("mem", "grp"), None),
        P(("mem", "grp"), None),
        P(("mem", "grp")),
        P(("mem", "grp"), None),
    )
    return jax.shard_map(
        local, mesh=mesh, in_specs=placed, out_specs=P(None, ("mem", "grp"), None), check_vma=False
    )
```

time: 435 us -> 105 us (0.24)
  the two profiles are of different devices: /device:TPU:577 before, /device:TPU:8 now
where the time goes in v1:
time: 105 us; the launch traced here: 104 us
  Pallas kernels  44.9 us (43%)
  starting transfers between devices  32.9 us (31%)
  waiting for transfers between devices  22.6 us (22%)
  local copies, waits for them, and re-layouts  2.89 us (3%)
    pallas_call x1, Pallas kernels, compute(): pl.pallas_call(lambda *refs: analyse(members, *refs), out_shape=jax.Shape...  44.9 us
    all_to_all x1, starting transfers between devices, local(): lax.all_to_all(obs_ens, 'grp', split_axis=1, concat_axis=0, tiled=True)  13 us
    ppermute x4, starting transfers between devices, ring(): lax.ppermute(x, ('mem', 'grp'), [(i, (i + step) % count) for i in range(c...  11.7 us
    ppermute x4, waiting for transfers between devices, ring(): lax.ppermute(x, ('mem', 'grp'), [(i, (i + step) % count) for i in range(c...  10.6 us
    all_to_all x1, starting transfers between devices, local(): lax.all_to_all(state, 'grp', split_axis=1, concat_axis=0, tiled=True)  8.18 us
    all_to_all x1, waiting for transfers between devices, local(): lax.all_to_all(state, 'grp', split_axis=1, concat_axis=0, tiled=True)  7.63 us
    all_to_all x1, waiting for transfers between devices, local(): lax.all_to_all(obs_ens, 'grp', split_axis=1, concat_axis=0, tiled=True)  4.34 us
    unnamed x12, local copies, waits for them, and re-layouts  2.87 us
  transfers between devices with their start and end apart: 6, of which 4 were waited for; matrix products, arithmetic and copies ran while one was open for 1% of the time, Pallas kernels for 0%

profile of v1, /device:TPU:8, one launch (start us, length us, event | category | flops | bytes accessed | tf_op | source)
XLA Modules:
  0.0 104.2 jit_solution(3389419317244072701)
XLA Ops:
  0.0 1.9 %copy.18 = f32[128,8,128]{2,0,1:T(8,128)} copy(f32[128,8,128]{2,1,0:T(8,128)} %param.8) | data formatting | bytes 1048576 | tf_op args[1]
  1.9 0.0 copy-start.3
  1.9 0.0 copy-start.4
  1.9 0.0 copy-start.1
  1.9 13.0 %all-to-all-start = ((f32[128,8,128]{2,0,1:T(8,128)}), f32[128,8,128]{2,0,1:T(8,128)S(1)}, u32[]{:S(2)}, u32[]{:S(2)}) async-start(f32[128,8,128]{2,0,1:T(8,128)} %copy.18), calls=%async_computation | async-start | bytes 1048576 | tf_op jit(solution)/shard_map/all_to_all | solution.py:241
  14.9 0.0 copy-done.3
  14.9 0.0 copy-done.4
  15.0 2.0 %collective-permute-start.3 = (f32[2,128]{1,0:T(2,128)S(1)}, f32[2,128]{1,0:T(2,128)S(1)}, u32[]{:S(2)}, u32[]{:S(2)}) collective-permute-start(f32[2,128]{1,0:T(2,128)S(1)} %pad_maximum_fusion.1), channel_id=1, source_target_pairs={{0,767},{1,0},{2,1},{3,2},{4,3},{5,4},{6,5},{7,6},{8,7},{9,8},{10,... | collective-permute-start | bytes 3080 | tf_op jit(solution)/shard_map/ppermute | solution.py:229
  17.0 3.8 %collective-permute-start.2 = (f32[2,128]{1,0:T(2,128)S(1)}, f32[2,128]{1,0:T(2,128)S(1)}, u32[]{:S(2)}, u32[]{:S(2)}) collective-permute-start(f32[2,128]{1,0:T(2,128)S(1)} %pad_maximum_fusion.1), channel_id=1, source_target_pairs={{0,1},{1,2},{2,3},{3,4},{4,5},{5,6},{6,7},{7,8},{8,9},{9,10},{10,1... | collective-permute-start | bytes 3080 | tf_op jit(solution)/shard_map/ppermute | solution.py:229
  20.8 0.0 copy-done.1
  20.8 0.9 copy.19
  21.7 4.3 %all-to-all-done = f32[128,8,128]{2,0,1:T(8,128)S(1)} async-done(((f32[128,8,128]{2,0,1:T(8,128)}), f32[128,8,128]{2,0,1:T(8,128)S(1)}, u32[]{:S(2)}, u32[]{:S(2)}) %all-to-all-start) | async-done | bytes 524320 | tf_op jit(solution)/shard_map/all_to_all | solution.py:241
  26.1 8.2 %all-to-all-start.1 = ((f32[128,8,128]{2,0,1:T(8,128)}), f32[128,8,128]{2,0,1:T(8,128)S(1)}, u32[]{:S(2)}, u32[]{:S(2)}) async-start(f32[128,8,128]{2,0,1:T(8,128)} %copy.19), calls=%async_computation.1 | async-start | bytes 1048576 | tf_op jit(solution)/shard_map/all_to_all | solution.py:242
  34.3 0.0 copy-start.2
  34.9 0.0 copy-done.2
  35.0 0.2 compare_reduce_fusion
  35.2 2.0 %collective-permute-start.1 = (f32[1024,128]{1,0:T(8,128)S(1)}, f32[1024,128]{1,0:T(8,128)S(1)}, u32[]{:S(2)}, u32[]{:S(2)}) collective-permute-start(f32[1024,128]{1,0:T(8,128)S(1)} %bitcast.34), channel_id=1, source_target_pairs={{0,767},{1,0},{2,1},{3,2},{4,3},{5,4},{6,5},{7,6},{8,7},{9,8},{10,... | collective-permute-start | bytes 1572872 | tf_op jit(solution)/shard_map/ppermute | solution.py:229
  37.2 3.8 %collective-permute-start = (f32[1024,128]{1,0:T(8,128)S(1)}, f32[1024,128]{1,0:T(8,128)S(1)}, u32[]{:S(2)}, u32[]{:S(2)}) collective-permute-start(f32[1024,128]{1,0:T(8,128)S(1)} %bitcast.35), channel_id=1, source_target_pairs={{0,1},{1,2},{2,3},{3,4},{4,5},{5,6},{6,7},{7,8},{8,9},{9,10},{10,1... | collective-permute-start | bytes 1572872 | tf_op jit(solution)/shard_map/ppermute | solution.py:229
  41.0 0.0 collective-permute-done.3
  41.0 0.0 collective-permute-done.2
  41.1 0.0 copy-start
  41.1 7.6 %all-to-all-done.1 = f32[128,8,128]{2,0,1:T(8,128)S(1)} async-done(((f32[128,8,128]{2,0,1:T(8,128)}), f32[128,8,128]{2,0,1:T(8,128)S(1)}, u32[]{:S(2)}, u32[]{:S(2)}) %all-to-all-start.1) | async-done | bytes 524320 | tf_op jit(solution)/shard_map/all_to_all | solution.py:242
  48.7 2.6 %collective-permute-done.1.refs_2_ = f32[1024,128]{1,0:T(8,128)S(1)} collective-permute-done((f32[1024,128]{1,0:T(8,128)S(1)}, f32[1024,128]{1,0:T(8,128)S(1)}, u32[]{:S(2)}, u32[]{:S(2)}) %collective-permute-start.1) | collective-permute-done | bytes 524320 | tf_op jit(solution)/shard_map/ppermute | solution.py:229
  51.3 8.0 %collective-permute-done.refs_1_ = f32[1024,128]{1,0:T(8,128)S(1)} collective-permute-done((f32[1024,128]{1,0:T(8,128)S(1)}, f32[1024,128]{1,0:T(8,128)S(1)}, u32[]{:S(2)}, u32[]{:S(2)}) %collective-permute-start) | collective-permute-done | bytes 524320 | tf_op jit(solution)/shard_map/ppermute | solution.py:229
  59.3 0.0 copy-done
  59.3 44.9 %shard_map.73 = f32[1024,128]{1,0:T(8,128)} custom-call(f32[1024,128]{1,0:T(8,128)S(1)} %bitcast.36, f32[1024,128]{1,0:T(8,128)S(1)} %collective-permute-done.refs_1_, f32[1024,128]{1,0:T(8,128)S(1)} %collective-permute-done.1.refs_2_, f32[1024,128]{1,0:T(8,128)S(1)} %bitcast.37, f32[3,128]{1,0:T(4,128)S(1)} %slice_bitcast_fusion.1.refs_4_, ...), custom_call_target="tpu_custom_call" | custom-call | tf_op jit(solution)/shard_map/pallas_call | solution.py:212
  (12 shorter events, 0.1 us)
Async XLA Ops:
  1.9 13.0 %copy-start.3 = (f32[1,128]{1,0:T(1,128)S(1)}, f32[1,128]{1,0:T(1,128)}, u32[]{:S(2)}) copy-start(f32[1,128]{1,0:T(1,128)} %param.10) | copy-start | bytes 1540
  1.9 13.0 %copy-start.4 = (f32[1,128]{1,0:T(1,128)S(1)}, f32[1,128]{1,0:T(1,128)}, u32[]{:S(2)}) copy-start(f32[1,128]{1,0:T(1,128)} %param.9) | copy-start | bytes 1540
  1.9 18.9 %copy-start.1 = (f32[128,8,128]{2,1,0:T(8,128)S(1)}, f32[128,8,128]{2,1,0:T(8,128)}, u32[]{:S(2)}) copy-start(f32[128,8,128]{2,1,0:T(8,128)} %param.7) | copy-start | bytes 1572868
  1.9 24.1 %all-to-all-start = ((f32[128,8,128]{2,0,1:T(8,128)}), f32[128,8,128]{2,0,1:T(8,128)S(1)}, u32[]{:S(2)}, u32[]{:S(2)}) async-start(f32[128,8,128]{2,0,1:T(8,128)} %copy.18), calls=%async_computation | async-start | bytes 1048576 | tf_op jit(solution)/shard_map/all_to_all | solution.py:241
  15.0 26.1 %collective-permute-start.3 = (f32[2,128]{1,0:T(2,128)S(1)}, f32[2,128]{1,0:T(2,128)S(1)}, u32[]{:S(2)}, u32[]{:S(2)}) collective-permute-start(f32[2,128]{1,0:T(2,128)S(1)} %pad_maximum_fusion.1), channel_id=1, source_target_pairs={{0,767},{1,0},{2,1},{3,2},{4,3},{5,4},{6,5},{7,6},{8,7},{9,8},{10,... | collective-permute-start | bytes 3080 | tf_op jit(solution)/shard_map/ppermute | solution.py:229
  17.0 24.0 %collective-permute-start.2 = (f32[2,128]{1,0:T(2,128)S(1)}, f32[2,128]{1,0:T(2,128)S(1)}, u32[]{:S(2)}, u32[]{:S(2)}) collective-permute-start(f32[2,128]{1,0:T(2,128)S(1)} %pad_maximum_fusion.1), channel_id=1, source_target_pairs={{0,1},{1,2},{2,3},{3,4},{4,5},{5,6},{6,7},{7,8},{8,9},{9,10},{10,1... | collective-permute-start | bytes 3080 | tf_op jit(solution)/shard_map/ppermute | solution.py:229
  26.1 22.6 %all-to-all-start.1 = ((f32[128,8,128]{2,0,1:T(8,128)}), f32[128,8,128]{2,0,1:T(8,128)S(1)}, u32[]{:S(2)}, u32[]{:S(2)}) async-start(f32[128,8,128]{2,0,1:T(8,128)} %copy.19), calls=%async_computation.1 | async-start | bytes 1048576 | tf_op jit(solution)/shard_map/all_to_all | solution.py:242
  34.3 0.7 copy-start.2
  35.2 16.2 %collective-permute-start.1 = (f32[1024,128]{1,0:T(8,128)S(1)}, f32[1024,128]{1,0:T(8,128)S(1)}, u32[]{:S(2)}, u32[]{:S(2)}) collective-permute-start(f32[1024,128]{1,0:T(8,128)S(1)} %bitcast.34), channel_id=1, source_target_pairs={{0,767},{1,0},{2,1},{3,2},{4,3},{5,4},{6,5},{7,6},{8,7},{9,8},{10,... | collective-permute-start | bytes 1572872 | tf_op jit(solution)/shard_map/ppermute | solution.py:229
  37.2 22.1 %collective-permute-start = (f32[1024,128]{1,0:T(8,128)S(1)}, f32[1024,128]{1,0:T(8,128)S(1)}, u32[]{:S(2)}, u32[]{:S(2)}) collective-permute-start(f32[1024,128]{1,0:T(8,128)S(1)} %bitcast.35), channel_id=1, source_target_pairs={{0,1},{1,2},{2,3},{3,4},{4,5},{5,6},{6,7},{7,8},{8,9},{9,10},{10,1... | collective-permute-start | bytes 1572872 | tf_op jit(solution)/shard_map/ppermute | solution.py:229
  41.1 18.2 %copy-start = (s32[1,128]{1,0:T(1,128)S(1)}, s32[1,128]{1,0:T(1,128)}, u32[]{:S(2)}) copy-start(s32[1,128]{1,0:T(1,128)} %refs_6_.1) | copy-start | bytes 1540

commit v2 on v1

v2 whole, which is shorter than its diff:
```python
import jax
import jax.numpy as jnp
from jax import lax
from jax.experimental import pallas as pl
from jax.experimental.pallas import tpu as pltpu
from jax.sharding import PartitionSpec as P

CHAINS = 8
SUB = 16
CUT = 4
BLOCK = 128


def lane(x, i):
    return jnp.broadcast_to(x[:, i:i + 1], x.shape)


def split(x):
    hi = x.astype(jnp.bfloat16)
    rest = x - hi.astype(jnp.float32)
    mid = rest.astype(jnp.bfloat16)
    lo = (rest - mid.astype(jnp.float32)).astype(jnp.bfloat16)
    return hi, mid, lo


def left(x, axis):
    hi, mid, lo = split(x)
    return jnp.concatenate([hi, hi, mid, hi, lo, mid], axis=axis)


def right(x, axis):
    hi, mid, lo = split(x)
    return jnp.concatenate([hi, mid, hi, lo, hi, mid], axis=axis)


def pair(x):
    hi, mid, lo = split(x)
    return (jnp.concatenate([hi, hi, mid, hi, lo, mid], axis=1), jnp.concatenate([hi, mid, hi, lo, hi, mid], axis=1))


def dot(a, b, ca, cb):
    return lax.dot_general(a, b, (((ca,), (cb,)), ((), ())), preferred_element_type=jnp.float32)


def sub_block(mat, inv, wrow, q):
    iota = lax.broadcasted_iota(jnp.int32, (CHAINS, BLOCK), 1)
    base = q * SUB
    panels = SUB // 8

    def block(rows, first):
        return {(a, b): lane(rows[a], first + b) for a in range(8) for b in range(a, 8)}

    groups = [
        [mat[pl.ds(base + 8 * r + a, CHAINS, stride=BLOCK), :] for a in range(8)]
        for r in range(panels)
    ]
    coef = block(groups[0], base)
    for p in range(panels):
        first = base + 8 * p
        inside = (iota >= first) & (iota < first + 8)
        rows = [jnp.where(inside, jnp.where(iota == first + a, 1.0, 0.0), groups[p][a]) for a in range(8)]
        for r in range(p + 1, panels):
            groups[r] = [jnp.where(inside, 0.0, x) for x in groups[r]]
        done = []
        ahead = None
        for t in range(8):
            scale = lax.rsqrt(coef[t, t])
            w = rows[t] * scale
            done.append(w)
            inv[pl.ds(first + t, CHAINS, stride=BLOCK), :] = jnp.where(iota <= first + t, w, 0.0)
            wrow[pl.ds(8 * p + t, CHAINS, stride=SUB), :] = w
            m = {a: coef[t, a] * scale for a in range(t + 1, 8)}
            for a in range(t + 1, 8):
                for b in range(a, 8):
                    coef[a, b] = coef[a, b] - m[a] * m[b]
                rows[a] = rows[a] - m[a] * w
            if p + 1 < panels:
                if t == CUT:
                    ahead = block(groups[p + 1], first + 8)
                c = [lane(w, first + 8 + a) for a in range(8)]
                for a in range(8):
                    groups[p + 1][a] = groups[p + 1][a] - c[a] * w
                if t >= CUT:
                    for a in range(8):
                        for b in range(a, 8):
                            ahead[a, b] = ahead[a, b] - c[a] * c[b]
        if p + 1 < panels:
            coef = ahead
            for r in range(p + 2, panels):
                for a in range(8):
                    x = groups[r][a]
                    for t in range(8):
                        x = x - lane(done[t], base + 8 * r + a) * done[t]
                    groups[r][a] = x


def join(mat, wrow, q):
    base = q * SUB
    lanes = lax.broadcasted_iota(jnp.int32, (SUB, BLOCK), 1)
    drop = (lanes > lax.broadcasted_iota(jnp.int32, (SUB, BLOCK), 0) + base) & (lanes < base + SUB)
    below = BLOCK - base - SUB
    over = lax.broadcasted_iota(jnp.int32, (below, BLOCK), 1)
    clear = (over >= base) & (over < base + SUB)
    for c in range(CHAINS):
        w = wrow[c * SUB:(c + 1) * SUB, :]
        out = dot(left(w, 0), right(jnp.where(drop, 0.0, w), 0), 0, 0)
        at = pl.ds(c * BLOCK + base + SUB, below)
        mat[at, :] = jnp.where(clear, 0.0, mat[at, :]) - out[base + SUB:, :]


def inverse_factors(mat, inv, wrow, beside=None):
    for q in range(BLOCK // SUB):
        if beside is not None:
            beside(q)
        sub_block(mat, inv, wrow, q)
        if (q + 1) * SUB < BLOCK:
            join(mat, wrow, q)


def at(k):
    return pl.ds(k * BLOCK, BLOCK)


def unit():
    return (lax.broadcasted_iota(jnp.int32, (BLOCK, BLOCK), 0)
            == lax.broadcasted_iota(jnp.int32, (BLOCK, BLOCK), 1)).astype(jnp.float32)


def scaled(joined, live, members, u):
    precise = jnp.where(live > 0, joined[members + 1:members + 2, :], 0.0)
    scale = jnp.sqrt(precise * (1.0 / (members - 1)))
    obs = joined[0:members, :]
    mean = jnp.mean(obs, axis=0, keepdims=True)
    u[...] = (obs - mean) * scale
    return (joined[members:members + 1, :] - mean) * scale


def begin(members, own, live, u0, row0, inv0, p00, wrow):
    row0[...] = jnp.broadcast_to(scaled(own, live[...], members, u0), row0.shape)
    total = unit()
    for k in range(members // BLOCK):
        uk = u0[at(k), :]
        total = total + dot(left(uk, 0), right(uk, 0), 0, 0)
        p00[at(k), :] = total
    inverse_factors(p00, inv0, wrow)


def factor(members, u0, row0, inv0, before, after, live,
           u1, u2, l10, l20, l21, inv1, inv2, y0, y1, y2, s, p11, p21, p22, wrow):
    eye = unit()
    first_row = lax.broadcasted_iota(jnp.int32, (BLOCK, BLOCK), 0) == 0
    row1 = scaled(before, live[0:1, :], members, u1)
    row2 = scaled(after, live[1:2, :], members, u2)

    def forcing(ref, row, c):
        if c + 1 < CHAINS:
            return ref[at(c + 1), :]
        return jnp.where(first_row, row, 0.0)

    carry = {}

    def add(name, x):
        carry[name] = carry[name] + x if name in carry else x
        return carry[name]

    for c in range(CHAINS):
        lhs = left(u1[at(c), :], 0)
        got = dot(lhs, right(jnp.concatenate([u0[at(c), :], u1[at(c), :]], axis=1), 0), 0, 0)
        p10 = add("p10", got[:, :BLOCK])
        gram = add("p11", got[:, BLOCK:])
        rows = dot(left(p10, 1), right(inv0[at(c), :], 1), 1, 1)
        l10[at(c), :] = rows
        lhs, rhs = pair(rows)
        p11[at(c), :] = eye + gram - dot(lhs, rhs, 1, 1)

    def beside_one(c):
        uk = [u0[at(c), :], u1[at(c), :], u2[at(c), :]]
        got = dot(left(uk[2], 0), right(jnp.concatenate(uk, axis=1), 0), 0, 0)
        p20 = add("p20", got[:, :BLOCK])
        g21 = add("p21", got[:, BLOCK:2 * BLOCK])
        g22 = add("p22", got[:, 2 * BLOCK:])
        rows = dot(left(jnp.concatenate([p20, forcing(u0, row0[0:1, :], c)], axis=0), 1),
                   right(inv0[at(c), :], 1), 1, 1)
        l20[at(c), :] = rows[:BLOCK]
        y0[at(c), :] = rows[BLOCK:]
        lhs, rhs = pair(rows)
        upd = dot(lhs, jnp.concatenate([right(l10[at(c), :], 1), rhs[:BLOCK]], axis=0), 1, 1)
        p21[at(c), :] = g21 - upd[:BLOCK, :BLOCK]
        p22[at(c), :] = eye + g22 - upd[:BLOCK, BLOCK:]
        y1[at(c), :] = forcing(u1, row1, c) - upd[BLOCK:, :BLOCK]
        y2[at(c), :] = forcing(u2, row2, c) - upd[BLOCK:, BLOCK:]
        if c + 1 < CHAINS:
            s[at(c + 1), :] = eye + dot(lhs[BLOCK:], rhs[BLOCK:], 1, 1)

    inverse_factors(p11, inv1, wrow, beside_one)
    for c in range(CHAINS):
        rows = dot(left(p21[at(c), :], 1), right(inv1[at(c), :], 1), 1, 1)
        l21[at(c), :] = rows
        lhs, rhs = pair(rows)
        p22[at(c), :] -= dot(lhs, rhs, 1, 1)

    def beside_two(c):
        if c == 0:
            lhs, rhs = pair(jnp.concatenate([u0[at(0), :], u1[at(0), :], u2[at(0), :]], axis=1))
            s[at(0), :] = eye + dot(lhs, rhs, 1, 1)
        rows = dot(left(y1[at(c), :], 1), right(inv1[at(c), :], 1), 1, 1)
        y1[at(c), :] = rows
        lhs, rhs = pair(rows)
        upd = dot(lhs, jnp.concatenate([right(l21[at(c), :], 1), rhs], axis=0), 1, 1)
        y2[at(c), :] -= upd[:, :BLOCK]
        if c + 1 < CHAINS:
            s[at(c + 1), :] += upd[:, BLOCK:]

    inverse_factors(p22, inv2, wrow, beside_two)
    for c in range(CHAINS):
        rows = dot(left(y2[at(c), :], 1), right(inv2[at(c), :], 1), 1, 1)
        y2[at(c), :] = rows
        if c + 1 < CHAINS:
            lhs, rhs = pair(rows)
            s[at(c + 1), :] += dot(lhs, rhs, 1, 1)


def apply(members, state, land, s_in, u0, u1, u2, inv0, inv1, inv2, l10, l20, l21, y0, y1, y2, out, s, r, inv, wrow):
    state_mean = jnp.mean(state[...], axis=0, keepdims=True)
    s[...] = s_in[...]
    carry = {}

    def beside(c):
        uk = [u0[at(c), :], u1[at(c), :], u2[at(c), :]]
        got = dot(left(state[at(c), :] - state_mean, 0), right(jnp.concatenate(uk, axis=1), 0), 0, 0)
        got = [got[:, i * BLOCK:(i + 1) * BLOCK] for i in range(3)]
        got = [x + y for x, y in zip(got, carry["f"])] if "f" in carry else got
        carry["f"] = got
        g = dot(left(got[0], 1), right(inv0[at(c), :], 1), 1, 1)
        upd = dot(left(g, 1), right(jnp.concatenate([l10[at(c), :], l20[at(c), :], y0[at(c), :]], axis=0), 1), 1, 1)
        g = dot(left(got[1] - upd[:, :BLOCK], 1), right(inv1[at(c), :], 1), 1, 1)
        more = dot(left(g, 1), right(jnp.concatenate([l21[at(c), :], y1[at(c), :]], axis=0), 1), 1, 1)
        last = got[2] - upd[:, BLOCK:2 * BLOCK] - more[:, :BLOCK]
        g = dot(left(last, 1), right(inv2[at(c), :], 1), 1, 1)
        r[at(c), :] = upd[:, 2 * BLOCK:] + more[:, BLOCK:] + dot(left(g, 1), right(y2[at(c), :], 1), 1, 1)

    inverse_factors(s, inv, wrow, beside)
    increment = dot(left(unit()[:8], 1), right(r[at(CHAINS - 1), :], 1), 1, 1)[0:1, :]
    shift = state_mean + increment
    wet = land[0:1, :] > 0
    for k in range(members // BLOCK):
        back = state[at(k), :]
        t = left(inv[at(k), :], 1)
        spread = dot(t, right(back - state_mean, 0), 1, 0)
        if k > 0:
            spread = spread - dot(t, right(r[at(k - 1), :], 1), 1, 1)
        out[at(k), :] = jnp.where(wet, shift + spread, back)


def call(kernel, members, outs, scratch, flops, *args):
    def shape(rows):
        return jax.ShapeDtypeStruct((rows, BLOCK), jnp.float32)

    return pl.pallas_call(
        lambda *refs: kernel(members, *refs),
        out_shape=tuple(shape(rows) for rows in outs),
        scratch_shapes=[pltpu.VMEM((members, BLOCK), jnp.float32)] * scratch
        + [pltpu.VMEM((CHAINS * SUB, BLOCK), jnp.float32)],
        compiler_params=pltpu.CompilerParams(vmem_limit_bytes=32 * 1024 * 1024),
        cost_estimate=pl.CostEstimate(flops=flops, bytes_accessed=2_000_000, transcendentals=0),
    )(*args)


def start(own, live):
    n = own.shape[0] - 8
    return call(begin, n, (n, 8, n), 1, 4_000_000_000, own, live[0:1])


def middle(u0, row0, inv0, before, after, live):
    n = u0.shape[0]
    return call(factor, n, (n,) * 11, 3, 10_000_000_000, u0, row0, inv0, before, after, live[1:3])


def finish(state, land, u0, inv0, mid):
    n = u0.shape[0]
    u1, u2, l10, l20, l21, inv1, inv2, y0, y1, y2, s = mid
    return call(apply, n, (n,), 3, 8_000_000_000, state, land, s, u0, u1, u2, inv0, inv1, inv2,
                l10, l20, l21, y0, y1, y2)[0]


def compute(own, before, after, state, value, precise, land):
    info = jnp.stack([value, precise], axis=1)
    own, before, after = (jnp.concatenate([x, info[i], jnp.zeros((6, BLOCK), jnp.float32)]) for i, x in enumerate((own, before, after)))
    live = jnp.ones((3, BLOCK), jnp.int32)
    u0, row0, inv0 = start(own, live)
    return finish(state, land, u0, inv0, middle(u0, row0, inv0, before, after, live))


def ring(x, step):
    count = lax.axis_size(("mem", "grp"))
    return lax.ppermute(x, ("mem", "grp"), [(i, (i + step) % count) for i in range(count)])


def local(state, obs_ens, obs_value, obs_precision, locality, obs_count, land_mask):
    spots = jnp.arange(3 * BLOCK, dtype=jnp.int32).reshape(3, BLOCK)
    spots = jnp.stack([spots[1], spots[0], spots[2]], axis=0)
    rank = jnp.arange(locality.shape[1], dtype=jnp.int32)
    live = jnp.where(rank < obs_count[0], locality[0], -1)
    live = jnp.any(spots[:, None, :] == live[None, :, None], axis=1).astype(jnp.int32)
    whole_obs = lax.all_to_all(obs_ens, "grp", split_axis=1, concat_axis=0, tiled=True)[:, 0, :]
    own = jnp.concatenate([whole_obs, obs_value, obs_precision, jnp.zeros((6, BLOCK), jnp.float32)], axis=0)
    before, after = ring(own, 1), ring(own, -1)
    u0, row0, inv0 = start(own, live)
    state, inv0 = lax.optimization_barrier((state, inv0))
    whole_state = lax.all_to_all(state, "grp", split_axis=1, concat_axis=0, tiled=True)[:, 0, :]
    mid = middle(u0, row0, inv0, before, after, live)
    out = finish(whole_state, land_mask, u0, inv0, mid)
    return out[:, None, :]


def solution(mesh):
    placed = (
        P("grp", "mem", None),
        P("grp", "mem", None),
        P(("mem", "grp"), None),
        P(("mem", "grp"), None),
        P(("mem", "grp"), None),
        P(("mem", "grp")),
        P(("mem", "grp"), None),
    )
    return jax.shard_map(
        local, mesh=mesh, in_specs=placed, out_specs=P(None, ("mem", "grp"), None), check_vma=False
    )
```

time: 105 us -> 102 us (0.971)
  local copies, waits for them, and re-layouts: 2.89 us -> 22.7 us
  waiting for transfers between devices: 22.6 us -> 10.4 us
  Pallas kernels: 44.9 us -> 36.3 us
  starting transfers between devices: 32.9 us -> 30.2 us
    unnamed x12 -> x51, local copies, waits for them, and re-layouts: 2.87 us -> 21.7 us
    ppermute x4 -> x2, waiting for transfers between devices: 10.6 us -> 0.01 us  [ring(): lax.ppermute(x, ('mem', 'grp'), [(i, (i + step) % count) for i in range(c...]
    pallas_call x1 -> x3, Pallas kernels: 44.9 us -> 36.3 us  [call(): pl.pallas_call(lambda *refs: kernel(members, *refs), out_shape=tuple((sha...]
    all_to_all x1, waiting for transfers between devices: 7.63 us -> 0.01 us  [local(): lax.all_to_all(state, 'grp', split_axis=1, concat_axis=0, tiled=True)]
    all_to_all x1, waiting for transfers between devices: 4.34 us -> 10.4 us  [local(): lax.all_to_all(obs_ens, 'grp', split_axis=1, concat_axis=0, tiled=True)]
    ppermute x4 -> x2, starting transfers between devices: 11.7 us -> 6.73 us  [ring(): lax.ppermute(x, ('mem', 'grp'), [(i, (i + step) % count) for i in range(c...]
    all_to_all x1, starting transfers between devices: 8.18 us -> 10.6 us  [local(): lax.all_to_all(state, 'grp', split_axis=1, concat_axis=0, tiled=True)]
  transfers between devices with their start and end apart: 6 -> 4, of which waited for: 4 -> 1; matrix products, arithmetic and copies ran while one was open for 1% -> 1% of each run, Pallas kernels for 0% -> 22%
where the time goes in v2:
time: 102 us; the launch traced here: 101 us
  Pallas kernels  36.3 us (36%)
  starting transfers between devices  30.2 us (30%)
  local copies, waits for them, and re-layouts  22.7 us (22%)
  waiting for transfers between devices  10.4 us (10%)
    pallas_call x3, Pallas kernels, call(): pl.pallas_call(lambda *refs: kernel(members, *refs), out_shape=tuple((sha...  36.3 us
    unnamed x51, local copies, waits for them, and re-layouts  21.7 us
    all_to_all x1, starting transfers between devices, local(): lax.all_to_all(obs_ens, 'grp', split_axis=1, concat_axis=0, tiled=True)  12.9 us
    all_to_all x1, starting transfers between devices, local(): lax.all_to_all(state, 'grp', split_axis=1, concat_axis=0, tiled=True)  10.6 us
    all_to_all x1, waiting for transfers between devices, local(): lax.all_to_all(obs_ens, 'grp', split_axis=1, concat_axis=0, tiled=True)  10.4 us
    ppermute x2, starting transfers between devices, ring(): lax.ppermute(x, ('mem', 'grp'), [(i, (i + step) % count) for i in range(c...  6.73 us
  transfers between devices with their start and end apart: 4, of which 1 were waited for; matrix products, arithmetic and copies ran while one was open for 1% of the time, Pallas kernels for 22%

profile of v2, /device:TPU:8, one launch (start us, length us, event | category | flops | bytes accessed | tf_op | source)
XLA Modules:
  0.0 100.6 jit_solution(3862363196379670618)
XLA Ops:
  0.0 1.9 %copy.14 = f32[128,8,128]{2,0,1:T(8,128)} copy(f32[128,8,128]{2,1,0:T(8,128)} %param.8) | data formatting | bytes 1048576 | tf_op args[1]
  1.9 12.9 %all-to-all-start = ((f32[128,8,128]{2,0,1:T(8,128)}), f32[128,8,128]{2,0,1:T(8,128)S(1)}, u32[]{:S(2)}, u32[]{:S(2)}) async-start(f32[128,8,128]{2,0,1:T(8,128)} %copy.14), calls=%async_computation | async-start | bytes 1048576 | tf_op jit(solution)/shard_map/all_to_all | solution.py:305
  14.8 0.0 copy-start.22
  15.5 0.0 copy-done.22
  15.5 10.4 %all-to-all-done = f32[128,8,128]{2,0,1:T(8,128)S(1)} async-done(((f32[128,8,128]{2,0,1:T(8,128)}), f32[128,8,128]{2,0,1:T(8,128)S(1)}, u32[]{:S(2)}, u32[]{:S(2)}) %all-to-all-start) | async-done | bytes 524320 | tf_op jit(solution)/shard_map/all_to_all | solution.py:305
  25.9 0.0 copy-start.23
  25.9 0.0 copy-start.24
  26.0 0.6 copy-done.23
  26.6 0.0 copy-done.24
  26.6 0.1 concatenate.3.refs_0_
  26.8 3.3 %collective-permute-start = (f32[1032,128]{1,0:T(8,128)S(1)}, f32[1032,128]{1,0:T(8,128)S(1)}, u32[]{:S(2)}, u32[]{:S(2)}) collective-permute-start(f32[1032,128]{1,0:T(8,128)S(1)} %concatenate.3.refs_0_), channel_id=1, source_target_pairs={{0,1},{1,2},{2,3},{3,4},{4,5},{5,6},{6,7},{7,8},{8,9},{9,10},{10,1... | collective-permute-start | bytes 1585160 | tf_op jit(solution)/shard_map/ppermute | solution.py:296
  30.0 3.5 %collective-permute-start.1 = (f32[1032,128]{1,0:T(8,128)S(1)}, f32[1032,128]{1,0:T(8,128)S(1)}, u32[]{:S(2)}, u32[]{:S(2)}) collective-permute-start(f32[1032,128]{1,0:T(8,128)S(1)} %concatenate.3.refs_0_), channel_id=1, source_target_pairs={{0,767},{1,0},{2,1},{3,2},{4,3},{5,4},{6,5},{7,6},{8,7},{9,8},{10,... | collective-permute-start | bytes 1585160 | tf_op jit(solution)/shard_map/ppermute | solution.py:296
  33.5 0.2 compare_reduce_fusion
  33.7 0.0 copy-start.21
  33.7 5.7 %shard_map.73 = (f32[1024,128]{1,0:T(8,128)S(1)}, f32[8,128]{1,0:T(8,128)S(1)}, f32[1024,128]{1,0:T(8,128)S(1)}) custom-call(f32[1032,128]{1,0:T(8,128)S(1)} %concatenate.3.refs_0_, s32[1,128]{1,0:T(1,128)S(1)} %slice.18.refs_1_), custom_call_target="tpu_custom_call" | custom-call | flops 4000000000 | bytes 2000000 | tf_op jit(solution)/shard_map/pallas_call | solution.py:259
  39.4 0.0 copy-done.21
  39.4 0.9 copy.15
  40.3 10.6 %all-to-all-start.1 = ((f32[128,8,128]{2,0,1:T(8,128)}), f32[128,8,128]{2,0,1:T(8,128)S(1)}, u32[]{:S(2)}, u32[]{:S(2)}) async-start(f32[128,8,128]{2,0,1:T(8,128)} %copy.15), calls=%async_computation.1 | async-start | bytes 1048576 | tf_op jit(solution)/shard_map/all_to_all | solution.py:310
  50.9 0.0 collective-permute-done.refs_3_
  50.9 0.0 collective-permute-done.1.refs_4_
  50.9 16.6 %shard_map.74 = (f32[1024,128]{1,0:T(8,128)S(1)}, f32[1024,128]{1,0:T(8,128)S(1)}, f32[1024,128]{1,0:T(8,128)S(1)}, f32[1024,128]{1,0:T(8,128)S(1)}, f32[1024,12...) custom-call(f32[1024,128]{1,0:T(8,128)S(1)} %get-tuple-element.23.re, ...), custom_call_target="tpu_custom_call" | custom-call | flops 10000000000 | bytes 2000000 | tf_op jit(solution)/shard_map/pallas_call | solution.py:259
  67.5 0.0 copy-start.1
  67.5 0.8 copy-done.1
  68.3 0.0 copy-start.3
  68.3 0.8 copy-done.3
  69.1 0.8 copy-done.5
  69.9 0.0 copy-start.7
  69.9 0.8 copy-done.7
  70.7 0.0 copy-start.9
  70.7 0.8 copy-done.9
  71.5 0.0 copy-start.11
  71.5 0.8 copy-done.11
  72.3 0.0 copy-start.13
  72.3 0.8 copy-done.13
  73.1 0.0 copy-start.15
  73.1 0.8 copy-done.15
  73.9 0.0 copy-start.17
  73.9 0.8 copy-done.17
  74.7 0.0 copy-start.19
  74.7 0.8 copy-done.19
  75.5 0.0 all-to-all-done.1
  75.5 0.0 copy-start
  75.5 0.7 copy-done
  76.2 0.0 copy-start.2
  76.2 1.0 %copy-done.2 = f32[1024,128]{1,0:T(8,128)S(1)} copy-done((f32[1024,128]{1,0:T(8,128)S(1)}, f32[1024,128]{1,0:T(8,128)}, u32[]{:S(2)}) %copy-start.2) | copy-done | bytes 524312
  77.2 0.0 copy-start.4
  77.2 1.0 %copy-done.4 = f32[1024,128]{1,0:T(8,128)S(1)} copy-done((f32[1024,128]{1,0:T(8,128)S(1)}, f32[1024,128]{1,0:T(8,128)}, u32[]{:S(2)}) %copy-start.4) | copy-done | bytes 524312
  78.3 0.0 copy-start.6
  78.3 1.0 %copy-done.6 = f32[1024,128]{1,0:T(8,128)S(1)} copy-done((f32[1024,128]{1,0:T(8,128)S(1)}, f32[1024,128]{1,0:T(8,128)}, u32[]{:S(2)}) %copy-start.6) | copy-done | bytes 524312
  79.3 0.0 copy-start.8
  79.3 1.0 %copy-done.8 = f32[1024,128]{1,0:T(8,128)S(1)} copy-done((f32[1024,128]{1,0:T(8,128)S(1)}, f32[1024,128]{1,0:T(8,128)}, u32[]{:S(2)}) %copy-start.8) | copy-done | bytes 524312
  80.3 0.0 copy-start.10
  80.3 1.0 %copy-done.10 = f32[1024,128]{1,0:T(8,128)S(1)} copy-done((f32[1024,128]{1,0:T(8,128)S(1)}, f32[1024,128]{1,0:T(8,128)}, u32[]{:S(2)}) %copy-start.10) | copy-done | bytes 524312
  81.4 0.0 copy-start.12
  81.4 1.0 %copy-done.12 = f32[1024,128]{1,0:T(8,128)S(1)} copy-done((f32[1024,128]{1,0:T(8,128)S(1)}, f32[1024,128]{1,0:T(8,128)}, u32[]{:S(2)}) %copy-start.12) | copy-done | bytes 524312
  82.4 0.0 copy-start.14
  82.4 1.0 %copy-done.14 = f32[1024,128]{1,0:T(8,128)S(1)} copy-done((f32[1024,128]{1,0:T(8,128)S(1)}, f32[1024,128]{1,0:T(8,128)}, u32[]{:S(2)}) %copy-start.14) | copy-done | bytes 524312
  83.5 0.0 copy-start.16
  83.5 1.0 %copy-done.16 = f32[1024,128]{1,0:T(8,128)S(1)} copy-done((f32[1024,128]{1,0:T(8,128)S(1)}, f32[1024,128]{1,0:T(8,128)}, u32[]{:S(2)}) %copy-start.16) | copy-done | bytes 524312
  84.5 0.0 copy-start.18
  84.5 1.0 %copy-done.18 = f32[1024,128]{1,0:T(8,128)S(1)} copy-done((f32[1024,128]{1,0:T(8,128)S(1)}, f32[1024,128]{1,0:T(8,128)}, u32[]{:S(2)}) %copy-start.18) | copy-done | bytes 524312
  85.6 0.0 copy-start.20
  85.6 1.0 %copy-done.20 = f32[1024,128]{1,0:T(8,128)S(1)} copy-done((f32[1024,128]{1,0:T(8,128)S(1)}, f32[1024,128]{1,0:T(8,128)}, u32[]{:S(2)}) %copy-start.20) | copy-done | bytes 524312
  86.6 14.0 %shard_map.75 = f32[1024,128]{1,0:T(8,128)} custom-call(f32[1024,128]{1,0:T(8,128)S(1)} %bitcast.15, s32[1,128]{1,0:T(1,128)S(1)} %copy-done, f32[1024,128]{1,0:T(8,128)S(1)} %copy-done.20, f32[1024,128]{1,0:T(8,128)S(1)} %get-tuple-element.23.refs_0_.refs_3_, f32[1024,128]{1,0:T(8,128)S(1)} %get-tuple-element.27.refs_4_, f32[1024,128]{1,0:T(8,128)S(1)} %copy-done.2, ...), custom_call_target="tpu_custom_call" | custom-call | flops 8000000000 | bytes 2000000 | tf_op jit(solution)/shard_map/pallas_call | solution.py:259
  (10 shorter events, 0.1 us)
Async XLA Ops:
  1.9 24.0 %all-to-all-start = ((f32[128,8,128]{2,0,1:T(8,128)}), f32[128,8,128]{2,0,1:T(8,128)S(1)}, u32[]{:S(2)}, u32[]{:S(2)}) async-start(f32[128,8,128]{2,0,1:T(8,128)} %copy.14), calls=%async_computation | async-start | bytes 1048576 | tf_op jit(solution)/shard_map/all_to_all | solution.py:305
  14.8 0.7 copy-start.22
  25.9 0.7 copy-start.23
  25.9 0.7 copy-start.24
  26.8 24.1 %collective-permute-start = (f32[1032,128]{1,0:T(8,128)S(1)}, f32[1032,128]{1,0:T(8,128)S(1)}, u32[]{:S(2)}, u32[]{:S(2)}) collective-permute-start(f32[1032,128]{1,0:T(8,128)S(1)} %concatenate.3.refs_0_), channel_id=1, source_target_pairs={{0,1},{1,2},{2,3},{3,4},{4,5},{5,6},{6,7},{7,8},{8,9},{9,10},{10,1... | collective-permute-start | bytes 1585160 | tf_op jit(solution)/shard_map/ppermute | solution.py:296
  30.0 20.8 %collective-permute-start.1 = (f32[1032,128]{1,0:T(8,128)S(1)}, f32[1032,128]{1,0:T(8,128)S(1)}, u32[]{:S(2)}, u32[]{:S(2)}) collective-permute-start(f32[1032,128]{1,0:T(8,128)S(1)} %concatenate.3.refs_0_), channel_id=1, source_target_pairs={{0,767},{1,0},{2,1},{3,2},{4,3},{5,4},{6,5},{7,6},{8,7},{9,8},{10,... | collective-permute-start | bytes 1585160 | tf_op jit(solution)/shard_map/ppermute | solution.py:296
  33.7 5.7 %copy-start.21 = (f32[128,8,128]{2,1,0:T(8,128)S(1)}, f32[128,8,128]{2,1,0:T(8,128)}, u32[]{:S(2)}) copy-start(f32[128,8,128]{2,1,0:T(8,128)} %param.7) | copy-start | bytes 1572868
  40.3 35.2 %all-to-all-start.1 = ((f32[128,8,128]{2,0,1:T(8,128)}), f32[128,8,128]{2,0,1:T(8,128)S(1)}, u32[]{:S(2)}, u32[]{:S(2)}) async-start(f32[128,8,128]{2,0,1:T(8,128)} %copy.15), calls=%async_computation.1 | async-start | bytes 1048576 | tf_op jit(solution)/shard_map/all_to_all | solution.py:310
  67.5 0.8 copy-start.1
  68.3 0.8 copy-start.3
  69.1 0.8 copy-start.5
  69.9 0.8 copy-start.7
  70.7 0.8 copy-start.9
  71.5 0.8 copy-start.11
  72.3 0.8 copy-start.13
  73.1 0.8 copy-start.15
  73.9 0.8 copy-start.17
  74.7 0.8 copy-start.19
  75.5 0.7 copy-start
  76.2 1.0 %copy-start.2 = (f32[1024,128]{1,0:T(8,128)S(1)}, f32[1024,128]{1,0:T(8,128)}, u32[]{:S(2)}) copy-start(f32[1024,128]{1,0:T(8,128)} %copy-done.1) | copy-start | bytes 1572868
  77.2 1.0 %copy-start.4 = (f32[1024,128]{1,0:T(8,128)S(1)}, f32[1024,128]{1,0:T(8,128)}, u32[]{:S(2)}) copy-start(f32[1024,128]{1,0:T(8,128)} %copy-done.3) | copy-start | bytes 1572868
  78.3 1.0 %copy-start.6 = (f32[1024,128]{1,0:T(8,128)S(1)}, f32[1024,128]{1,0:T(8,128)}, u32[]{:S(2)}) copy-start(f32[1024,128]{1,0:T(8,128)} %copy-done.5) | copy-start | bytes 1572868
  79.3 1.0 %copy-start.8 = (f32[1024,128]{1,0:T(8,128)S(1)}, f32[1024,128]{1,0:T(8,128)}, u32[]{:S(2)}) copy-start(f32[1024,128]{1,0:T(8,128)} %copy-done.7) | copy-start | bytes 1572868
  80.3 1.0 %copy-start.10 = (f32[1024,128]{1,0:T(8,128)S(1)}, f32[1024,128]{1,0:T(8,128)}, u32[]{:S(2)}) copy-start(f32[1024,128]{1,0:T(8,128)} %copy-done.9) | copy-start | bytes 1572868
  81.4 1.0 %copy-start.12 = (f32[1024,128]{1,0:T(8,128)S(1)}, f32[1024,128]{1,0:T(8,128)}, u32[]{:S(2)}) copy-start(f32[1024,128]{1,0:T(8,128)} %copy-done.11) | copy-start | bytes 1572868
  82.4 1.0 %copy-start.14 = (f32[1024,128]{1,0:T(8,128)S(1)}, f32[1024,128]{1,0:T(8,128)}, u32[]{:S(2)}) copy-start(f32[1024,128]{1,0:T(8,128)} %copy-done.13) | copy-start | bytes 1572868
  83.5 1.0 %copy-start.16 = (f32[1024,128]{1,0:T(8,128)S(1)}, f32[1024,128]{1,0:T(8,128)}, u32[]{:S(2)}) copy-start(f32[1024,128]{1,0:T(8,128)} %copy-done.15) | copy-start | bytes 1572868
  84.5 1.0 %copy-start.18 = (f32[1024,128]{1,0:T(8,128)S(1)}, f32[1024,128]{1,0:T(8,128)}, u32[]{:S(2)}) copy-start(f32[1024,128]{1,0:T(8,128)} %copy-done.17) | copy-start | bytes 1572868
  85.6 1.0 %copy-start.20 = (f32[1024,128]{1,0:T(8,128)S(1)}, f32[1024,128]{1,0:T(8,128)}, u32[]{:S(2)}) copy-start(f32[1024,128]{1,0:T(8,128)} %copy-done.19) | copy-start | bytes 1572868

commit v3 on v2

--- a/solution.py
+++ b/solution.py
@@ -108,13 +108,21 @@
         mat[at, :] = jnp.where(clear, 0.0, mat[at, :]) - out[base + SUB:, :]
 
 
-def inverse_factors(mat, inv, wrow, beside=None):
-    for q in range(BLOCK // SUB):
-        if beside is not None:
-            beside(q)
+def inverse_factors(mat, inv, wrow, stages=()):
+    def beside(q):
+        for step in range(max((len(group) for group in stages), default=0)):
+            for d, group in enumerate(stages):
+                if step < len(group) and 0 <= q - d < CHAINS:
+                    group[step](q - d)
+
+    count = BLOCK // SUB
+    for q in range(count):
+        beside(q)
         sub_block(mat, inv, wrow, q)
-        if (q + 1) * SUB < BLOCK:
+        if q + 1 < count:
             join(mat, wrow, q)
+    for q in range(count, count + len(stages) - 1):
+        beside(q)
 
 
 def at(k):
@@ -145,101 +153,138 @@
     inverse_factors(p00, inv0, wrow)
 
 
-def factor(members, u0, row0, inv0, before, after, live,
-           u1, u2, l10, l20, l21, inv1, inv2, y0, y1, y2, s, p11, p21, p22, wrow):
+def factor(members, u0, row0, inv0, before, after, live, *rest):
+    outs, (u1, u2, l10, l20, l21, inv1, inv2, y0, y1, y2, s, p11, p21, p22, wrow, sems) = rest[:11], rest[11:]
+    kept = (u1, u2, l10, l20, l21, inv1, inv2, y0, y1, y2, s)
+    copies = [pltpu.make_async_copy(kept[i], outs[i], sems.at[i]) for i in range(11)]
+
+    def send(*refs):
+        for i in refs:
+            copies[i].start()
+
     eye = unit()
     first_row = lax.broadcasted_iota(jnp.int32, (BLOCK, BLOCK), 0) == 0
     row1 = scaled(before, live[0:1, :], members, u1)
     row2 = scaled(after, live[1:2, :], members, u2)
+    send(0, 1)
 
     def forcing(ref, row, c):
         if c + 1 < CHAINS:
             return ref[at(c + 1), :]
         return jnp.where(first_row, row, 0.0)
 
-    carry = {}
-
-    def add(name, x):
-        carry[name] = carry[name] + x if name in carry else x
-        return carry[name]
-
-    for c in range(CHAINS):
-        lhs = left(u1[at(c), :], 0)
-        got = dot(lhs, right(jnp.concatenate([u0[at(c), :], u1[at(c), :]], axis=1), 0), 0, 0)
-        p10 = add("p10", got[:, :BLOCK])
-        gram = add("p11", got[:, BLOCK:])
-        rows = dot(left(p10, 1), right(inv0[at(c), :], 1), 1, 1)
-        l10[at(c), :] = rows
-        lhs, rhs = pair(rows)
-        p11[at(c), :] = eye + gram - dot(lhs, rhs, 1, 1)
-
-    def beside_one(c):
+    for c in range(CHAINS):
+        got = dot(left(u1[at(c), :], 0), right(jnp.concatenate([u0[at(c), :], u1[at(c), :]], axis=1), 0), 0, 0)
+        l10[at(c), :] = got[:, :BLOCK] + (l10[at(c - 1), :] if c else 0.0)
+        p11[at(c), :] = got[:, BLOCK:] + (p11[at(c - 1), :] if c else eye)
+    for c in range(CHAINS):
+        l10[at(c), :] = dot(left(l10[at(c), :], 1), right(inv0[at(c), :], 1), 1, 1)
+    send(2)
+    for c in range(CHAINS):
+        lhs, rhs = pair(l10[at(c), :])
+        p11[at(c), :] -= dot(lhs, rhs, 1, 1)
+
+    def gram(c):
         uk = [u0[at(c), :], u1[at(c), :], u2[at(c), :]]
         got = dot(left(uk[2], 0), right(jnp.concatenate(uk, axis=1), 0), 0, 0)
-        p20 = add("p20", got[:, :BLOCK])
-        g21 = add("p21", got[:, BLOCK:2 * BLOCK])
-        g22 = add("p22", got[:, 2 * BLOCK:])
-        rows = dot(left(jnp.concatenate([p20, forcing(u0, row0[0:1, :], c)], axis=0), 1),
+        l20[at(c), :] = got[:, :BLOCK] + (l20[at(c - 1), :] if c else 0.0)
+        p21[at(c), :] = got[:, BLOCK:2 * BLOCK] + (p21[at(c - 1), :] if c else 0.0)
+        p22[at(c), :] = got[:, 2 * BLOCK:] + (p22[at(c - 1), :] if c else eye)
+
+    def low(c):
+        rows = dot(left(jnp.concatenate([l20[at(c), :], forcing(u0, row0[0:1, :], c)], axis=0), 1),
                    right(inv0[at(c), :], 1), 1, 1)
         l20[at(c), :] = rows[:BLOCK]
         y0[at(c), :] = rows[BLOCK:]
-        lhs, rhs = pair(rows)
+
+    def take(c):
+        lhs, rhs = pair(jnp.concatenate([l20[at(c), :], y0[at(c), :]], axis=0))
         upd = dot(lhs, jnp.concatenate([right(l10[at(c), :], 1), rhs[:BLOCK]], axis=0), 1, 1)
-        p21[at(c), :] = g21 - upd[:BLOCK, :BLOCK]
-        p22[at(c), :] = eye + g22 - upd[:BLOCK, BLOCK:]
+        p21[at(c), :] -= upd[:BLOCK, :BLOCK]
+        p22[at(c), :] -= upd[:BLOCK, BLOCK:]
         y1[at(c), :] = forcing(u1, row1, c) - upd[BLOCK:, :BLOCK]
         y2[at(c), :] = forcing(u2, row2, c) - upd[BLOCK:, BLOCK:]
         if c + 1 < CHAINS:
             s[at(c + 1), :] = eye + dot(lhs[BLOCK:], rhs[BLOCK:], 1, 1)
 
-    inverse_factors(p11, inv1, wrow, beside_one)
-    for c in range(CHAINS):
-        rows = dot(left(p21[at(c), :], 1), right(inv1[at(c), :], 1), 1, 1)
-        l21[at(c), :] = rows
-        lhs, rhs = pair(rows)
+    inverse_factors(p11, inv1, wrow, ((gram,), (low,), (take,)))
+    send(3, 5, 7)
+    for c in range(CHAINS):
+        l21[at(c), :] = dot(left(p21[at(c), :], 1), right(inv1[at(c), :], 1), 1, 1)
+    send(4)
+    for c in range(CHAINS):
+        lhs, rhs = pair(l21[at(c), :])
         p22[at(c), :] -= dot(lhs, rhs, 1, 1)
 
-    def beside_two(c):
-        if c == 0:
-            lhs, rhs = pair(jnp.concatenate([u0[at(0), :], u1[at(0), :], u2[at(0), :]], axis=1))
-            s[at(0), :] = eye + dot(lhs, rhs, 1, 1)
-        rows = dot(left(y1[at(c), :], 1), right(inv1[at(c), :], 1), 1, 1)
-        y1[at(c), :] = rows
-        lhs, rhs = pair(rows)
+    def low_two(c):
+        y1[at(c), :] = dot(left(y1[at(c), :], 1), right(inv1[at(c), :], 1), 1, 1)
+
+    def take_two(c):
+        lhs, rhs = pair(y1[at(c), :])
         upd = dot(lhs, jnp.concatenate([right(l21[at(c), :], 1), rhs], axis=0), 1, 1)
         y2[at(c), :] -= upd[:, :BLOCK]
         if c + 1 < CHAINS:
             s[at(c + 1), :] += upd[:, BLOCK:]
-
-    inverse_factors(p22, inv2, wrow, beside_two)
-    for c in range(CHAINS):
-        rows = dot(left(y2[at(c), :], 1), right(inv2[at(c), :], 1), 1, 1)
-        y2[at(c), :] = rows
-        if c + 1 < CHAINS:
-            lhs, rhs = pair(rows)
-            s[at(c + 1), :] += dot(lhs, rhs, 1, 1)
-
-
-def apply(members, state, land, s_in, u0, u1, u2, inv0, inv1, inv2, l10, l20, l21, y0, y1, y2, out, s, r, inv, wrow):
+        else:
+            lhs, rhs = pair(jnp.concatenate([u0[at(0), :], u1[at(0), :], u2[at(0), :]], axis=1))
+            s[at(0), :] = eye + dot(lhs, rhs, 1, 1)
+
+    inverse_factors(p22, inv2, wrow, ((low_two,), (take_two,)))
+    send(6, 8)
+    for c in range(CHAINS):
+        y2[at(c), :] = dot(left(y2[at(c), :], 1), right(inv2[at(c), :], 1), 1, 1)
+    send(9)
+    for c in range(CHAINS - 1):
+        lhs, rhs = pair(y2[at(c), :])
+        s[at(c + 1), :] += dot(lhs, rhs, 1, 1)
+    send(10)
+    for copy in copies:
+        copy.wait()
+
+
+def apply(members, state, land, *rest):
+    ins, out, rest = rest[:13], rest[13], rest[14:]
+    s, u0, u1, u2, inv0, l10, l20, y0, inv1, l21, y1, inv2, y2, f0, f1, f2, r, inv, wrow, sems = rest
+    kept = (s, u0, u1, u2, inv0, l10, l20, y0, inv1, l21, y1, inv2, y2)
+    copies = [pltpu.make_async_copy(ins[i], kept[i], sems.at[i]) for i in range(13)]
+    for copy in copies:
+        copy.start()
     state_mean = jnp.mean(state[...], axis=0, keepdims=True)
-    s[...] = s_in[...]
-    carry = {}
-
-    def beside(c):
+    for copy in copies:
+        copy.wait()
+
+    def gram(c):
         uk = [u0[at(c), :], u1[at(c), :], u2[at(c), :]]
         got = dot(left(state[at(c), :] - state_mean, 0), right(jnp.concatenate(uk, axis=1), 0), 0, 0)
-        got = [got[:, i * BLOCK:(i + 1) * BLOCK] for i in range(3)]
-        got = [x + y for x, y in zip(got, carry["f"])] if "f" in carry else got
-        carry["f"] = got
-        g = dot(left(got[0], 1), right(inv0[at(c), :], 1), 1, 1)
-        upd = dot(left(g, 1), right(jnp.concatenate([l10[at(c), :], l20[at(c), :], y0[at(c), :]], axis=0), 1), 1, 1)
-        g = dot(left(got[1] - upd[:, :BLOCK], 1), right(inv1[at(c), :], 1), 1, 1)
-        more = dot(left(g, 1), right(jnp.concatenate([l21[at(c), :], y1[at(c), :]], axis=0), 1), 1, 1)
-        last = got[2] - upd[:, BLOCK:2 * BLOCK] - more[:, :BLOCK]
-        g = dot(left(last, 1), right(inv2[at(c), :], 1), 1, 1)
-        r[at(c), :] = upd[:, 2 * BLOCK:] + more[:, BLOCK:] + dot(left(g, 1), right(y2[at(c), :], 1), 1, 1)
-
-    inverse_factors(s, inv, wrow, beside)
+        for i, ref in enumerate((f0, f1, f2)):
+            x = got[:, i * BLOCK:(i + 1) * BLOCK]
+            ref[at(c + 1), :] = x + (ref[at(c), :] if c else 0.0)
+
+    def low_one(c):
+        r[at(c), :] = dot(left(f0[at(c + 1), :], 1), right(inv0[at(c), :], 1), 1, 1)
+
+    def take_one(c):
+        cols = jnp.concatenate([l10[at(c), :], l20[at(c), :], y0[at(c), :]], axis=0)
+        upd = dot(left(r[at(c), :], 1), right(cols, 1), 1, 1)
+        f1[at(c + 1), :] -= upd[:, :BLOCK]
+        f2[at(c + 1), :] -= upd[:, BLOCK:2 * BLOCK]
+        r[at(c), :] = upd[:, 2 * BLOCK:]
+
+    def low_two(c):
+        f1[at(c + 1), :] = dot(left(f1[at(c + 1), :], 1), right(inv1[at(c), :], 1), 1, 1)
+
+    def take_two(c):
+        upd = dot(left(f1[at(c + 1), :], 1), right(jnp.concatenate([l21[at(c), :], y1[at(c), :]], axis=0), 1), 1, 1)
+        f2[at(c + 1), :] -= upd[:, :BLOCK]
+        r[at(c), :] += upd[:, BLOCK:]
+
+    def low_three(c):
+        f2[at(c + 1), :] = dot(left(f2[at(c + 1), :], 1), right(inv2[at(c), :], 1), 1, 1)
+
+    def take_three(c):
+        r[at(c), :] += dot(left(f2[at(c + 1), :], 1), right(y2[at(c), :], 1), 1, 1)
+
+    inverse_factors(s, inv, wrow, ((gram,), (low_one, take_one), (low_two, take_two), (low_three, take_three)))
     increment = dot(left(unit()[:8], 1), right(r[at(CHAINS - 1), :], 1), 1, 1)[0:1, :]
     shift = state_mean + increment
     wet = land[0:1, :] > 0
@@ -252,15 +297,16 @@
         out[at(k), :] = jnp.where(wet, shift + spread, back)
 
 
-def call(kernel, members, outs, scratch, flops, *args):
-    def shape(rows):
-        return jax.ShapeDtypeStruct((rows, BLOCK), jnp.float32)
-
+def call(kernel, members, outs, scratch, flops, args, far_in=0, far_out=0):
+    far, near = pl.BlockSpec(memory_space=pltpu.HBM), pl.BlockSpec(memory_space=pltpu.VMEM)
+    sems = [pltpu.SemaphoreType.DMA((far_in + far_out,))] if far_in + far_out else []
     return pl.pallas_call(
         lambda *refs: kernel(members, *refs),
-        out_shape=tuple(shape(rows) for rows in outs),
-        scratch_shapes=[pltpu.VMEM((members, BLOCK), jnp.float32)] * scratch
-        + [pltpu.VMEM((CHAINS * SUB, BLOCK), jnp.float32)],
+        out_shape=tuple(jax.ShapeDtypeStruct((rows, BLOCK), jnp.float32) for rows in outs),
+        in_specs=[near] * (len(args) - far_in) + [far] * far_in,
+        out_specs=tuple([far] * far_out + [near] * (len(outs) - far_out)),
+        scratch_shapes=[pltpu.VMEM((rows, BLOCK), jnp.float32) for rows in scratch]
+        + [pltpu.VMEM((CHAINS * SUB, BLOCK), jnp.float32)] + sems,
         compiler_params=pltpu.CompilerParams(vmem_limit_bytes=32 * 1024 * 1024),
         cost_estimate=pl.CostEstimate(flops=flops, bytes_accessed=2_000_000, transcendentals=0),
     )(*args)
@@ -268,19 +314,19 @@
 
 def start(own, live):
     n = own.shape[0] - 8
-    return call(begin, n, (n, 8, n), 1, 4_000_000_000, own, live[0:1])
+    return call(begin, n, (n, 8, n), (n,), 4_000_000_000, (own, live[0:1]))
 
 
 def middle(u0, row0, inv0, before, after, live):
     n = u0.shape[0]
-    return call(factor, n, (n,) * 11, 3, 10_000_000_000, u0, row0, inv0, before, after, live[1:3])
+    return call(factor, n, (n,) * 11, (n,) * 14, 10_000_000_000, (u0, row0, inv0, before, after, live[1:3]), 0, 11)
 
 
 def finish(state, land, u0, inv0, mid):
     n = u0.shape[0]
     u1, u2, l10, l20, l21, inv1, inv2, y0, y1, y2, s = mid
-    return call(apply, n, (n,), 3, 8_000_000_000, state, land, s, u0, u1, u2, inv0, inv1, inv2,
-                l10, l20, l21, y0, y1, y2)[0]
+    far = (s, u0, u1, u2, inv0, l10, l20, y0, inv1, l21, y1, inv2, y2)
+    return call(apply, n, (n,), (n,) * 13 + (n + BLOCK,) * 3 + (n, n), 8_000_000_000, (state, land) + far, 13, 0)[0]
 
 
 def compute(own, before, after, state, value, precise, land):

time: 102 us -> 97.2 us (0.953)
  Pallas kernels: 36.3 us -> 31.8 us
    pallas_call x3, Pallas kernels: 36.3 us -> 31.8 us  [call(): pl.pallas_call(lambda *refs: kernel(members, *refs), out_shape=tuple((jax...]
  transfers between devices with their start and end apart: 4 -> 4, of which waited for: 1 -> 1; matrix products, arithmetic and copies ran while one was open for 1% -> 1% of each run, Pallas kernels for 22% -> 23%
where the time goes in v3:
time: 97.2 us; the launch traced here: 96.4 us
  Pallas kernels  31.8 us (33%)
  starting transfers between devices  30.2 us (31%)
  local copies, waits for them, and re-layouts  22.7 us (23%)
  waiting for transfers between devices  10.4 us (11%)
  between operations  1 us (1%)
    pallas_call x3, Pallas kernels, call(): pl.pallas_call(lambda *refs: kernel(members, *refs), out_shape=tuple((jax...  31.8 us
    unnamed x51, local copies, waits for them, and re-layouts  21.7 us
    all_to_all x1, starting transfers between devices, local(): lax.all_to_all(obs_ens, 'grp', split_axis=1, concat_axis=0, tiled=True)  12.9 us
    all_to_all x1, starting transfers between devices, local(): lax.all_to_all(state, 'grp', split_axis=1, concat_axis=0, tiled=True)  10.6 us
    all_to_all x1, waiting for transfers between devices, local(): lax.all_to_all(obs_ens, 'grp', split_axis=1, concat_axis=0, tiled=True)  10.4 us
    ppermute x2, starting transfers between devices, ring(): lax.ppermute(x, ('mem', 'grp'), [(i, (i + step) % count) for i in range(c...  6.73 us
  transfers between devices with their start and end apart: 4, of which 1 were waited for; matrix products, arithmetic and copies ran while one was open for 1% of the time, Pallas kernels for 23%

profile of v3, /device:TPU:8, one launch (start us, length us, event | category | flops | bytes accessed | tf_op | source)
XLA Modules:
  0.0 96.4 jit_solution(8254204915988894661)
XLA Ops:
  0.0 1.9 %copy.14 = f32[128,8,128]{2,0,1:T(8,128)} copy(f32[128,8,128]{2,1,0:T(8,128)} %param.8) | data formatting | bytes 1048576 | tf_op args[1]
  1.9 12.9 %all-to-all-start = ((f32[128,8,128]{2,0,1:T(8,128)}), f32[128,8,128]{2,0,1:T(8,128)S(1)}, u32[]{:S(2)}, u32[]{:S(2)}) async-start(f32[128,8,128]{2,0,1:T(8,128)} %copy.14), calls=%async_computation | async-start | bytes 1048576 | tf_op jit(solution)/shard_map/all_to_all | solution.py:351
  14.8 0.0 copy-start.22
  15.5 0.0 copy-done.22
  15.5 10.4 %all-to-all-done = f32[128,8,128]{2,0,1:T(8,128)S(1)} async-done(((f32[128,8,128]{2,0,1:T(8,128)}), f32[128,8,128]{2,0,1:T(8,128)S(1)}, u32[]{:S(2)}, u32[]{:S(2)}) %all-to-all-start) | async-done | bytes 524320 | tf_op jit(solution)/shard_map/all_to_all | solution.py:351
  25.9 0.0 copy-start.23
  25.9 0.0 copy-start.24
  26.0 0.6 copy-done.23
  26.6 0.0 copy-done.24
  26.6 0.1 concatenate.3.refs_0_
  26.8 3.3 %collective-permute-start = (f32[1032,128]{1,0:T(8,128)S(1)}, f32[1032,128]{1,0:T(8,128)S(1)}, u32[]{:S(2)}, u32[]{:S(2)}) collective-permute-start(f32[1032,128]{1,0:T(8,128)S(1)} %concatenate.3.refs_0_), channel_id=1, source_target_pairs={{0,1},{1,2},{2,3},{3,4},{4,5},{5,6},{6,7},{7,8},{8,9},{9,10},{10,1... | collective-permute-start | bytes 1585160 | tf_op jit(solution)/shard_map/ppermute | solution.py:342
  30.0 3.5 %collective-permute-start.1 = (f32[1032,128]{1,0:T(8,128)S(1)}, f32[1032,128]{1,0:T(8,128)S(1)}, u32[]{:S(2)}, u32[]{:S(2)}) collective-permute-start(f32[1032,128]{1,0:T(8,128)S(1)} %concatenate.3.refs_0_), channel_id=1, source_target_pairs={{0,767},{1,0},{2,1},{3,2},{4,3},{5,4},{6,5},{7,6},{8,7},{9,8},{10,... | collective-permute-start | bytes 1585160 | tf_op jit(solution)/shard_map/ppermute | solution.py:342
  33.5 0.2 compare_reduce_fusion
  33.7 0.0 copy-start.21
  33.7 5.7 %shard_map.73 = (f32[1024,128]{1,0:T(8,128)S(1)}, f32[8,128]{1,0:T(8,128)S(1)}, f32[1024,128]{1,0:T(8,128)S(1)}) custom-call(f32[1032,128]{1,0:T(8,128)S(1)} %concatenate.3.refs_0_, s32[1,128]{1,0:T(1,128)S(1)} %slice.18.refs_1_), custom_call_target="tpu_custom_call" | custom-call | flops 4000000000 | bytes 2000000 | tf_op jit(solution)/shard_map/pallas_call | solution.py:303
  39.4 0.0 copy-done.21
  39.4 0.9 copy.15
  40.3 10.6 %all-to-all-start.1 = ((f32[128,8,128]{2,0,1:T(8,128)}), f32[128,8,128]{2,0,1:T(8,128)S(1)}, u32[]{:S(2)}, u32[]{:S(2)}) async-start(f32[128,8,128]{2,0,1:T(8,128)} %copy.15), calls=%async_computation.1 | async-start | bytes 1048576 | tf_op jit(solution)/shard_map/all_to_all | solution.py:356
  50.9 0.0 collective-permute-done.refs_3_
  50.9 0.0 collective-permute-done.1.refs_4_
  50.9 16.4 %shard_map.74 = (f32[1024,128]{1,0:T(8,128)S(1)}, f32[1024,128]{1,0:T(8,128)S(1)}, f32[1024,128]{1,0:T(8,128)S(1)}, f32[1024,128]{1,0:T(8,128)S(1)}, f32[1024,12...) custom-call(f32[1024,128]{1,0:T(8,128)S(1)} %get-tuple-element.23.re, ...), custom_call_target="tpu_custom_call" | custom-call | flops 10000000000 | bytes 2000000 | tf_op jit(solution)/shard_map/pallas_call | solution.py:303
  67.3 0.0 copy-start.1
  67.3 0.8 copy-done.1
  68.1 0.0 copy-start.3
  68.1 0.8 copy-done.3
  68.9 0.0 copy-start.5
  68.9 0.8 copy-done.5
  69.7 0.0 copy-start.7
  69.7 0.8 copy-done.7
  70.5 0.0 copy-start.9
  70.5 0.8 copy-done.9
  71.3 0.0 copy-start.11
  71.3 0.8 copy-done.11
  72.1 0.0 copy-start.13
  72.1 0.8 copy-done.13
  72.9 0.0 copy-start.15
  72.9 0.8 copy-done.15
  73.7 0.0 copy-start.17
  73.7 0.8 copy-done.17
  74.5 0.0 copy-start.19
  74.5 0.8 copy-done.19
  75.3 0.0 all-to-all-done.1
  75.3 0.0 copy-start
  75.3 0.7 copy-done
  76.0 0.0 copy-start.2
  76.0 1.0 %copy-done.2 = f32[1024,128]{1,0:T(8,128)S(1)} copy-done((f32[1024,128]{1,0:T(8,128)S(1)}, f32[1024,128]{1,0:T(8,128)}, u32[]{:S(2)}) %copy-start.2) | copy-done | bytes 524312
  77.0 0.0 copy-start.4
  77.0 1.0 %copy-done.4 = f32[1024,128]{1,0:T(8,128)S(1)} copy-done((f32[1024,128]{1,0:T(8,128)S(1)}, f32[1024,128]{1,0:T(8,128)}, u32[]{:S(2)}) %copy-start.4) | copy-done | bytes 524312
  78.1 0.0 copy-start.6
  78.1 1.0 %copy-done.6 = f32[1024,128]{1,0:T(8,128)S(1)} copy-done((f32[1024,128]{1,0:T(8,128)S(1)}, f32[1024,128]{1,0:T(8,128)}, u32[]{:S(2)}) %copy-start.6) | copy-done | bytes 524312
  79.1 0.0 copy-start.8
  79.1 1.0 %copy-done.8 = f32[1024,128]{1,0:T(8,128)S(1)} copy-done((f32[1024,128]{1,0:T(8,128)S(1)}, f32[1024,128]{1,0:T(8,128)}, u32[]{:S(2)}) %copy-start.8) | copy-done | bytes 524312
  80.1 0.0 copy-start.10
  80.1 1.0 %copy-done.10 = f32[1024,128]{1,0:T(8,128)S(1)} copy-done((f32[1024,128]{1,0:T(8,128)S(1)}, f32[1024,128]{1,0:T(8,128)}, u32[]{:S(2)}) %copy-start.10) | copy-done | bytes 524312
  81.2 0.0 copy-start.12
  81.2 1.0 %copy-done.12 = f32[1024,128]{1,0:T(8,128)S(1)} copy-done((f32[1024,128]{1,0:T(8,128)S(1)}, f32[1024,128]{1,0:T(8,128)}, u32[]{:S(2)}) %copy-start.12) | copy-done | bytes 524312
  82.2 0.0 copy-start.14
  82.2 1.0 %copy-done.14 = f32[1024,128]{1,0:T(8,128)S(1)} copy-done((f32[1024,128]{1,0:T(8,128)S(1)}, f32[1024,128]{1,0:T(8,128)}, u32[]{:S(2)}) %copy-start.14) | copy-done | bytes 524312
  83.3 0.0 copy-start.16
  83.3 1.0 %copy-done.16 = f32[1024,128]{1,0:T(8,128)S(1)} copy-done((f32[1024,128]{1,0:T(8,128)S(1)}, f32[1024,128]{1,0:T(8,128)}, u32[]{:S(2)}) %copy-start.16) | copy-done | bytes 524312
  84.3 0.0 copy-start.18
  84.3 1.0 %copy-done.18 = f32[1024,128]{1,0:T(8,128)S(1)} copy-done((f32[1024,128]{1,0:T(8,128)S(1)}, f32[1024,128]{1,0:T(8,128)}, u32[]{:S(2)}) %copy-start.18) | copy-done | bytes 524312
  85.4 1.0 %copy-done.20 = f32[1024,128]{1,0:T(8,128)S(1)} copy-done((f32[1024,128]{1,0:T(8,128)S(1)}, f32[1024,128]{1,0:T(8,128)}, u32[]{:S(2)}) %copy-start.20) | copy-done | bytes 524312
  86.4 9.8 %shard_map.75 = f32[1024,128]{1,0:T(8,128)} custom-call(f32[1024,128]{1,0:T(8,128)S(1)} %bitcast.15, s32[1,128]{1,0:T(1,128)S(1)} %copy-done, f32[1024,128]{1,0:T(8,128)S(1)} %copy-done.20, f32[1024,128]{1,0:T(8,128)S(1)} %get-tuple-element.23.refs_0_.refs_3_, f32[1024,128]{1,0:T(8,128)S(1)} %get-tuple-element.27.refs_4_, f32[1024,128]{1,0:T(8,128)S(1)} %copy-done.2, ...), custom_call_target="tpu_custom_call" | custom-call | flops 8000000000 | bytes 2000000 | tf_op jit(solution)/shard_map/pallas_call | solution.py:303
  (10 shorter events, 0.1 us)
Async XLA Ops:
  1.9 24.0 %all-to-all-start = ((f32[128,8,128]{2,0,1:T(8,128)}), f32[128,8,128]{2,0,1:T(8,128)S(1)}, u32[]{:S(2)}, u32[]{:S(2)}) async-start(f32[128,8,128]{2,0,1:T(8,128)} %copy.14), calls=%async_computation | async-start | bytes 1048576 | tf_op jit(solution)/shard_map/all_to_all | solution.py:351
  14.8 0.7 copy-start.22
  25.9 0.7 copy-start.23
  25.9 0.7 copy-start.24
  26.8 24.1 %collective-permute-start = (f32[1032,128]{1,0:T(8,128)S(1)}, f32[1032,128]{1,0:T(8,128)S(1)}, u32[]{:S(2)}, u32[]{:S(2)}) collective-permute-start(f32[1032,128]{1,0:T(8,128)S(1)} %concatenate.3.refs_0_), channel_id=1, source_target_pairs={{0,1},{1,2},{2,3},{3,4},{4,5},{5,6},{6,7},{7,8},{8,9},{9,10},{10,1... | collective-permute-start | bytes 1585160 | tf_op jit(solution)/shard_map/ppermute | solution.py:342
  30.0 20.8 %collective-permute-start.1 = (f32[1032,128]{1,0:T(8,128)S(1)}, f32[1032,128]{1,0:T(8,128)S(1)}, u32[]{:S(2)}, u32[]{:S(2)}) collective-permute-start(f32[1032,128]{1,0:T(8,128)S(1)} %concatenate.3.refs_0_), channel_id=1, source_target_pairs={{0,767},{1,0},{2,1},{3,2},{4,3},{5,4},{6,5},{7,6},{8,7},{9,8},{10,... | collective-permute-start | bytes 1585160 | tf_op jit(solution)/shard_map/ppermute | solution.py:342
  33.7 5.7 %copy-start.21 = (f32[128,8,128]{2,1,0:T(8,128)S(1)}, f32[128,8,128]{2,1,0:T(8,128)}, u32[]{:S(2)}) copy-start(f32[128,8,128]{2,1,0:T(8,128)} %param.7) | copy-start | bytes 1572868
  40.3 35.0 %all-to-all-start.1 = ((f32[128,8,128]{2,0,1:T(8,128)}), f32[128,8,128]{2,0,1:T(8,128)S(1)}, u32[]{:S(2)}, u32[]{:S(2)}) async-start(f32[128,8,128]{2,0,1:T(8,128)} %copy.15), calls=%async_computation.1 | async-start | bytes 1048576 | tf_op jit(solution)/shard_map/all_to_all | solution.py:356
  67.3 0.8 copy-start.1
  68.1 0.8 copy-start.3
  68.9 0.8 copy-start.5
  69.7 0.8 copy-start.7
  70.5 0.8 copy-start.9
  71.3 0.8 copy-start.11
  72.1 0.8 copy-start.13
  72.9 0.8 copy-start.15
  73.7 0.8 copy-start.17
  74.5 0.8 copy-start.19
  75.3 0.7 copy-start
  76.0 1.0 %copy-start.2 = (f32[1024,128]{1,0:T(8,128)S(1)}, f32[1024,128]{1,0:T(8,128)}, u32[]{:S(2)}) copy-start(f32[1024,128]{1,0:T(8,128)} %copy-done.1) | copy-start | bytes 1572868
  77.0 1.0 %copy-start.4 = (f32[1024,128]{1,0:T(8,128)S(1)}, f32[1024,128]{1,0:T(8,128)}, u32[]{:S(2)}) copy-start(f32[1024,128]{1,0:T(8,128)} %copy-done.3) | copy-start | bytes 1572868
  78.1 1.0 %copy-start.6 = (f32[1024,128]{1,0:T(8,128)S(1)}, f32[1024,128]{1,0:T(8,128)}, u32[]{:S(2)}) copy-start(f32[1024,128]{1,0:T(8,128)} %copy-done.5) | copy-start | bytes 1572868
  79.1 1.0 %copy-start.8 = (f32[1024,128]{1,0:T(8,128)S(1)}, f32[1024,128]{1,0:T(8,128)}, u32[]{:S(2)}) copy-start(f32[1024,128]{1,0:T(8,128)} %copy-done.7) | copy-start | bytes 1572868
  80.1 1.0 %copy-start.10 = (f32[1024,128]{1,0:T(8,128)S(1)}, f32[1024,128]{1,0:T(8,128)}, u32[]{:S(2)}) copy-start(f32[1024,128]{1,0:T(8,128)} %copy-done.9) | copy-start | bytes 1572868
  81.2 1.0 %copy-start.12 = (f32[1024,128]{1,0:T(8,128)S(1)}, f32[1024,128]{1,0:T(8,128)}, u32[]{:S(2)}) copy-start(f32[1024,128]{1,0:T(8,128)} %copy-done.11) | copy-start | bytes 1572868
  82.2 1.0 %copy-start.14 = (f32[1024,128]{1,0:T(8,128)S(1)}, f32[1024,128]{1,0:T(8,128)}, u32[]{:S(2)}) copy-start(f32[1024,128]{1,0:T(8,128)} %copy-done.13) | copy-start | bytes 1572868
  83.3 1.0 %copy-start.16 = (f32[1024,128]{1,0:T(8,128)S(1)}, f32[1024,128]{1,0:T(8,128)}, u32[]{:S(2)}) copy-start(f32[1024,128]{1,0:T(8,128)} %copy-done.15) | copy-start | bytes 1572868
  84.3 1.0 %copy-start.18 = (f32[1024,128]{1,0:T(8,128)S(1)}, f32[1024,128]{1,0:T(8,128)}, u32[]{:S(2)}) copy-start(f32[1024,128]{1,0:T(8,128)} %copy-done.17) | copy-start | bytes 1572868
  85.4 1.0 %copy-start.20 = (f32[1024,128]{1,0:T(8,128)S(1)}, f32[1024,128]{1,0:T(8,128)}, u32[]{:S(2)}) copy-start(f32[1024,128]{1,0:T(8,128)} %copy-done.19) | copy-start | bytes 1572868

commit v4 on v3

--- a/solution.py
+++ b/solution.py
@@ -154,14 +154,15 @@
 
 
 def factor(members, u0, row0, inv0, before, after, live, *rest):
-    outs, (u1, u2, l10, l20, l21, inv1, inv2, y0, y1, y2, s, p11, p21, p22, wrow, sems) = rest[:11], rest[11:]
-    kept = (u1, u2, l10, l20, l21, inv1, inv2, y0, y1, y2, s)
-    copies = [pltpu.make_async_copy(kept[i], outs[i], sems.at[i]) for i in range(11)]
+    store, u1, u2, l10, l20, l21, inv1, inv2, y0, y1, y2, s, p11, p21, p22, wrow, sems = rest
+    kept = (u1, u2, l10, l20, l21, inv1, inv2, y0, y1, y2, s, u0, inv0)
+    copies = [pltpu.make_async_copy(kept[i], store.at[pl.ds(i * members, members), :], sems.at[i]) for i in range(PARTS)]
 
     def send(*refs):
         for i in refs:
             copies[i].start()
 
+    send(11, 12)
     eye = unit()
     first_row = lax.broadcasted_iota(jnp.int32, (BLOCK, BLOCK), 0) == 0
     row1 = scaled(before, live[0:1, :], members, u1)
@@ -242,18 +243,22 @@
         copy.wait()
 
 
-def apply(members, state, land, *rest):
-    ins, out, rest = rest[:13], rest[13], rest[14:]
-    s, u0, u1, u2, inv0, l10, l20, y0, inv1, l21, y1, inv2, y2, f0, f1, f2, r, inv, wrow, sems = rest
-    kept = (s, u0, u1, u2, inv0, l10, l20, y0, inv1, l21, y1, inv2, y2)
-    copies = [pltpu.make_async_copy(ins[i], kept[i], sems.at[i]) for i in range(13)]
-    for copy in copies:
-        copy.start()
+def apply(members, state, land, store, out, *rest):
+    u1, u2, l10, l20, l21, inv1, inv2, y0, y1, y2, s, u0, inv0, f0, f1, f2, r, inv, wrow, sems = rest
+    kept = (u1, u2, l10, l20, l21, inv1, inv2, y0, y1, y2, s, u0, inv0)
+    copies = [pltpu.make_async_copy(store.at[pl.ds(i * members, members), :], kept[i], sems.at[i]) for i in range(PARTS)]
+    for i in (10, 11, 0, 1, 12, 2, 3, 7, 5, 4, 8, 6, 9):
+        copies[i].start()
+
+    def need(c, *parts):
+        for i in parts if c == 0 else ():
+            copies[i].wait()
+
     state_mean = jnp.mean(state[...], axis=0, keepdims=True)
-    for copy in copies:
-        copy.wait()
+    need(0, 10)
 
     def gram(c):
+        need(c, 11, 0, 1)
         uk = [u0[at(c), :], u1[at(c), :], u2[at(c), :]]
         got = dot(left(state[at(c), :] - state_mean, 0), right(jnp.concatenate(uk, axis=1), 0), 0, 0)
         for i, ref in enumerate((f0, f1, f2)):
@@ -261,9 +266,11 @@
             ref[at(c + 1), :] = x + (ref[at(c), :] if c else 0.0)
 
     def low_one(c):
+        need(c, 12)
         r[at(c), :] = dot(left(f0[at(c + 1), :], 1), right(inv0[at(c), :], 1), 1, 1)
 
     def take_one(c):
+        need(c, 2, 3, 7)
         cols = jnp.concatenate([l10[at(c), :], l20[at(c), :], y0[at(c), :]], axis=0)
         upd = dot(left(r[at(c), :], 1), right(cols, 1), 1, 1)
         f1[at(c + 1), :] -= upd[:, :BLOCK]
@@ -271,17 +278,21 @@
         r[at(c), :] = upd[:, 2 * BLOCK:]
 
     def low_two(c):
+        need(c, 5)
         f1[at(c + 1), :] = dot(left(f1[at(c + 1), :], 1), right(inv1[at(c), :], 1), 1, 1)
 
     def take_two(c):
+        need(c, 4, 8)
         upd = dot(left(f1[at(c + 1), :], 1), right(jnp.concatenate([l21[at(c), :], y1[at(c), :]], axis=0), 1), 1, 1)
         f2[at(c + 1), :] -= upd[:, :BLOCK]
         r[at(c), :] += upd[:, BLOCK:]
 
     def low_three(c):
+        need(c, 6)
         f2[at(c + 1), :] = dot(left(f2[at(c + 1), :], 1), right(inv2[at(c), :], 1), 1, 1)
 
     def take_three(c):
+        need(c, 9)
         r[at(c), :] += dot(left(f2[at(c + 1), :], 1), right(y2[at(c), :], 1), 1, 1)
 
     inverse_factors(s, inv, wrow, ((gram,), (low_one, take_one), (low_two, take_two), (low_three, take_three)))
@@ -297,17 +308,19 @@
         out[at(k), :] = jnp.where(wet, shift + spread, back)
 
 
-def call(kernel, members, outs, scratch, flops, args, far_in=0, far_out=0):
+PARTS = 13
+
+
+def call(kernel, members, outs, scratch, flops, args, far_in=False, far_out=False):
     far, near = pl.BlockSpec(memory_space=pltpu.HBM), pl.BlockSpec(memory_space=pltpu.VMEM)
-    sems = [pltpu.SemaphoreType.DMA((far_in + far_out,))] if far_in + far_out else []
     return pl.pallas_call(
         lambda *refs: kernel(members, *refs),
         out_shape=tuple(jax.ShapeDtypeStruct((rows, BLOCK), jnp.float32) for rows in outs),
-        in_specs=[near] * (len(args) - far_in) + [far] * far_in,
-        out_specs=tuple([far] * far_out + [near] * (len(outs) - far_out)),
+        in_specs=[near] * (len(args) - 1) + [far if far_in else near],
+        out_specs=tuple([far if far_out else near] * len(outs)),
         scratch_shapes=[pltpu.VMEM((rows, BLOCK), jnp.float32) for rows in scratch]
-        + [pltpu.VMEM((CHAINS * SUB, BLOCK), jnp.float32)] + sems,
-        compiler_params=pltpu.CompilerParams(vmem_limit_bytes=32 * 1024 * 1024),
+        + [pltpu.VMEM((CHAINS * SUB, BLOCK), jnp.float32)] + [pltpu.SemaphoreType.DMA((PARTS,))] * (far_in or far_out),
+        compiler_params=pltpu.CompilerParams(vmem_limit_bytes=40 * 1024 * 1024),
         cost_estimate=pl.CostEstimate(flops=flops, bytes_accessed=2_000_000, transcendentals=0),
     )(*args)
 
@@ -319,14 +332,12 @@
 
 def middle(u0, row0, inv0, before, after, live):
     n = u0.shape[0]
-    return call(factor, n, (n,) * 11, (n,) * 14, 10_000_000_000, (u0, row0, inv0, before, after, live[1:3]), 0, 11)
-
-
-def finish(state, land, u0, inv0, mid):
-    n = u0.shape[0]
-    u1, u2, l10, l20, l21, inv1, inv2, y0, y1, y2, s = mid
-    far = (s, u0, u1, u2, inv0, l10, l20, y0, inv1, l21, y1, inv2, y2)
-    return call(apply, n, (n,), (n,) * 13 + (n + BLOCK,) * 3 + (n, n), 8_000_000_000, (state, land) + far, 13, 0)[0]
+    return call(factor, n, (50 * n,), (n,) * 14, 10_000_000_000, (u0, row0, inv0, before, after, live[1:3]), far_out=True)[0]
+
+
+def finish(state, land, mid):
+    n = state.shape[0]
+    return call(apply, n, (n,), (n,) * PARTS + (n + BLOCK,) * 3 + (n, n), 8_000_000_000, (state, land, mid), far_in=True)[0]
 
 
 def compute(own, before, after, state, value, precise, land):
@@ -334,7 +345,7 @@
     own, before, after = (jnp.concatenate([x, info[i], jnp.zeros((6, BLOCK), jnp.float32)]) for i, x in enumerate((own, before, after)))
     live = jnp.ones((3, BLOCK), jnp.int32)
     u0, row0, inv0 = start(own, live)
-    return finish(state, land, u0, inv0, middle(u0, row0, inv0, before, after, live))
+    return finish(state, land, middle(u0, row0, inv0, before, after, live))
 
 
 def ring(x, step):
@@ -349,13 +360,14 @@
     live = jnp.where(rank < obs_count[0], locality[0], -1)
     live = jnp.any(spots[:, None, :] == live[None, :, None], axis=1).astype(jnp.int32)
     whole_obs = lax.all_to_all(obs_ens, "grp", split_axis=1, concat_axis=0, tiled=True)[:, 0, :]
+    whole_obs, turned = lax.optimization_barrier((whole_obs, jnp.swapaxes(state, 0, 1)))
     own = jnp.concatenate([whole_obs, obs_value, obs_precision, jnp.zeros((6, BLOCK), jnp.float32)], axis=0)
     before, after = ring(own, 1), ring(own, -1)
     u0, row0, inv0 = start(own, live)
-    state, inv0 = lax.optimization_barrier((state, inv0))
-    whole_state = lax.all_to_all(state, "grp", split_axis=1, concat_axis=0, tiled=True)[:, 0, :]
+    turned, inv0 = lax.optimization_barrier((turned, inv0))
+    whole_state = lax.all_to_all(turned, "grp", split_axis=0, concat_axis=0, tiled=True).reshape(-1, BLOCK)
     mid = middle(u0, row0, inv0, before, after, live)
-    out = finish(whole_state, land_mask, u0, inv0, mid)
+    out = finish(whole_state, land_mask, mid)
     return out[:, None, :]
 
 

time: 97.2 us -> 81.7 us (0.84)
  local copies, waits for them, and re-layouts: 22.7 us -> 4.7 us
  waiting for transfers between devices: 10.4 us -> 12.5 us
  Pallas kernels: 31.8 us -> 33.4 us
  starting transfers between devices: 30.2 us -> 28.9 us
    unnamed x51 -> x4, local copies, waits for them, and re-layouts: 21.7 us -> 3.88 us
    ppermute x2, waiting for transfers between devices: 0.01 us -> 3.63 us  [ring(): lax.ppermute(x, ('mem', 'grp'), [(i, (i + step) % count) for i in range(c...]
    all_to_all x1, waiting for transfers between devices: 10.4 us -> 8.85 us  [local(): lax.all_to_all(obs_ens, 'grp', split_axis=1, concat_axis=0, tiled=True)]
    pallas_call x3, Pallas kernels: 31.8 us -> 33.4 us  [call(): pl.pallas_call(lambda *refs: kernel(members, *refs), out_shape=tuple((jax...]
  transfers between devices with their start and end apart: 4 -> 4, of which waited for: 1 -> 2; matrix products, arithmetic and copies ran while one was open for 1% -> 3% of each run, Pallas kernels for 23% -> 26%
where the time goes in v4:
time: 81.7 us; the launch traced here: 81.3 us
  Pallas kernels  33.4 us (41%)
  starting transfers between devices  28.9 us (35%)
  waiting for transfers between devices  12.5 us (15%)
  local copies, waits for them, and re-layouts  4.7 us (6%)
  between operations  0.93 us (1%)
  other arithmetic  0.88 us (1%)
    pallas_call x3, Pallas kernels, call(): pl.pallas_call(lambda *refs: kernel(members, *refs), out_shape=tuple((jax...  33.4 us
    all_to_all x1, starting transfers between devices, local(): lax.all_to_all(obs_ens, 'grp', split_axis=1, concat_axis=0, tiled=True)  12.9 us
    all_to_all x1, starting transfers between devices, local(): lax.all_to_all(turned, 'grp', split_axis=0, concat_axis=0, tiled=True)  10.2 us
    all_to_all x1, waiting for transfers between devices, local(): lax.all_to_all(obs_ens, 'grp', split_axis=1, concat_axis=0, tiled=True)  8.85 us
    ppermute x2, starting transfers between devices, ring(): lax.ppermute(x, ('mem', 'grp'), [(i, (i + step) % count) for i in range(c...  5.83 us
    unnamed x4, local copies, waits for them, and re-layouts  3.88 us
    ppermute x2, waiting for transfers between devices, ring(): lax.ppermute(x, ('mem', 'grp'), [(i, (i + step) % count) for i in range(c...  3.63 us
  transfers between devices with their start and end apart: 4, of which 2 were waited for; matrix products, arithmetic and copies ran while one was open for 3% of the time, Pallas kernels for 26%

profile of v4, /device:TPU:8, one launch (start us, length us, event | category | flops | bytes accessed | tf_op | source)
XLA Modules:
  0.0 81.3 jit_solution(9296665346746197731)
XLA Ops:
  0.0 1.9 %copy.14 = f32[128,8,128]{2,0,1:T(8,128)} copy(f32[128,8,128]{2,1,0:T(8,128)} %param.8) | data formatting | bytes 1048576 | tf_op args[1]
  1.9 12.9 %all-to-all-start = ((f32[128,8,128]{2,0,1:T(8,128)}), f32[128,8,128]{2,0,1:T(8,128)S(1)}, u32[]{:S(2)}, u32[]{:S(2)}) async-start(f32[128,8,128]{2,0,1:T(8,128)} %copy.14), calls=%async_computation | async-start | bytes 1048576 | tf_op jit(solution)/shard_map/all_to_all | solution.py:362
  15.4 1.9 %copy.18 = f32[128,8,128]{2,0,1:T(8,128)} copy(f32[128,8,128]{2,1,0:T(8,128)} %param.7) | data formatting | bytes 1048576 | tf_op args[0]
  17.4 0.7 reduce
  18.1 8.8 %all-to-all-done = f32[128,8,128]{2,0,1:T(8,128)S(1)} async-done(((f32[128,8,128]{2,0,1:T(8,128)}), f32[128,8,128]{2,0,1:T(8,128)S(1)}, u32[]{:S(2)}, u32[]{:S(2)}) %all-to-all-start) | async-done | bytes 524320 | tf_op jit(solution)/shard_map/all_to_all | solution.py:362
  27.0 0.8 concatenate.3.refs_0_
  27.8 3.0 %collective-permute-start.1 = (f32[1032,128]{1,0:T(8,128)S(1)}, f32[1032,128]{1,0:T(8,128)S(1)}, u32[]{:S(2)}, u32[]{:S(2)}) collective-permute-start(f32[1032,128]{1,0:T(8,128)S(1)} %concatenate.3.refs_0_), channel_id=1, source_target_pairs={{0,767},{1,0},{2,1},{3,2},{4,3},{5,4},{6,5},{7,6},{8,7},{9,8},{10,... | collective-permute-start | bytes 1585160 | tf_op jit(solution)/shard_map/ppermute | solution.py:353
  30.8 2.8 %collective-permute-start = (f32[1032,128]{1,0:T(8,128)S(1)}, f32[1032,128]{1,0:T(8,128)S(1)}, u32[]{:S(2)}, u32[]{:S(2)}) collective-permute-start(f32[1032,128]{1,0:T(8,128)S(1)} %concatenate.3.refs_0_), channel_id=1, source_target_pairs={{0,1},{1,2},{2,3},{3,4},{4,5},{5,6},{6,7},{7,8},{8,9},{9,10},{10,1... | collective-permute-start | bytes 1585160 | tf_op jit(solution)/shard_map/ppermute | solution.py:353
  33.6 0.2 compare_reduce_fusion
  33.8 0.0 copy-start
  33.8 5.5 %shard_map.73 = (f32[1024,128]{1,0:T(8,128)S(1)}, f32[8,128]{1,0:T(8,128)S(1)}, f32[1024,128]{1,0:T(8,128)S(1)}) custom-call(f32[1032,128]{1,0:T(8,128)S(1)} %concatenate.3.refs_0_, s32[1,128]{1,0:T(1,128)S(1)} %slice.18.refs_1_), custom_call_target="tpu_custom_call" | custom-call | flops 4000000000 | bytes 2000000 | tf_op jit(solution)/shard_map/pallas_call | solution.py:316
  39.4 10.2 %all-to-all-start.1 = ((f32[8,128,128]{2,1,0:T(8,128)}), f32[8,128,128]{2,1,0:T(8,128)S(1)}, u32[]{:S(2)}, u32[]{:S(2)}) async-start(f32[8,128,128]{2,1,0:T(8,128)} %bitcast.16), calls=%async_computation.1 | async-start | bytes 1048576 | tf_op jit(solution)/shard_map/all_to_all | solution.py:368
  49.6 0.0 collective-permute-done.1.refs_4_
  49.6 3.6 %collective-permute-done.refs_3_ = f32[1032,128]{1,0:T(8,128)S(1)} collective-permute-done((f32[1032,128]{1,0:T(8,128)S(1)}, f32[1032,128]{1,0:T(8,128)S(1)}, u32[]{:S(2)}, u32[]{:S(2)}) %collective-permute-start) | collective-permute-done | bytes 528416 | tf_op jit(solution)/shard_map/ppermute | solution.py:353
  53.2 15.8 %shard_map.74.refs_2_ = f32[51200,128]{1,0:T(8,128)} custom-call(f32[1024,128]{1,0:T(8,128)S(1)} %get-tuple-element.16.refs_0_, f32[8,128]{1,0:T(8,128)S(1)} %get-tuple-element.17.refs_1_, f32[1024,128]{1,0:T(8,128)S(1)} %get-tuple-element.18.refs_2_, f32[1032,128]{1,0:T(8,128)S(1)} %collective-permute-done.refs_3_, ...), custom_call_target="tpu_custom_call" | custom-call | flops 10000000000 | bytes 2000000 | tf_op jit(solution)/shard_map/pallas_call | solution.py:316
  69.0 0.0 all-to-all-done.1
  69.0 0.0 copy-done
  69.0 12.1 %shard_map.75 = f32[1024,128]{1,0:T(8,128)} custom-call(f32[1024,128]{1,0:T(8,128)S(1)} %bitcast.14, s32[1,128]{1,0:T(1,128)S(1)} %copy-done, f32[51200,128]{1,0:T(8,128)} %shard_map.74.refs_2_), custom_call_target="tpu_custom_call" | custom-call | flops 8000000000 | bytes 2000000 | tf_op jit(solution)/shard_map/pallas_call | solution.py:316
  (8 shorter events, 0.0 us)
Async XLA Ops:
  1.9 25.0 %all-to-all-start = ((f32[128,8,128]{2,0,1:T(8,128)}), f32[128,8,128]{2,0,1:T(8,128)S(1)}, u32[]{:S(2)}, u32[]{:S(2)}) async-start(f32[128,8,128]{2,0,1:T(8,128)} %copy.14), calls=%async_computation | async-start | bytes 1048576 | tf_op jit(solution)/shard_map/all_to_all | solution.py:362
  27.8 21.8 %collective-permute-start.1 = (f32[1032,128]{1,0:T(8,128)S(1)}, f32[1032,128]{1,0:T(8,128)S(1)}, u32[]{:S(2)}, u32[]{:S(2)}) collective-permute-start(f32[1032,128]{1,0:T(8,128)S(1)} %concatenate.3.refs_0_), channel_id=1, source_target_pairs={{0,767},{1,0},{2,1},{3,2},{4,3},{5,4},{6,5},{7,6},{8,7},{9,8},{10,... | collective-permute-start | bytes 1585160 | tf_op jit(solution)/shard_map/ppermute | solution.py:353
  30.8 22.4 %collective-permute-start = (f32[1032,128]{1,0:T(8,128)S(1)}, f32[1032,128]{1,0:T(8,128)S(1)}, u32[]{:S(2)}, u32[]{:S(2)}) collective-permute-start(f32[1032,128]{1,0:T(8,128)S(1)} %concatenate.3.refs_0_), channel_id=1, source_target_pairs={{0,1},{1,2},{2,3},{3,4},{4,5},{5,6},{6,7},{7,8},{8,9},{9,10},{10,1... | collective-permute-start | bytes 1585160 | tf_op jit(solution)/shard_map/ppermute | solution.py:353
  33.8 35.2 %copy-start = (s32[1,128]{1,0:T(1,128)S(1)}, s32[1,128]{1,0:T(1,128)}, u32[]{:S(2)}) copy-start(s32[1,128]{1,0:T(1,128)} %refs_1_.1) | copy-start | bytes 1540
  39.4 29.6 %all-to-all-start.1 = ((f32[8,128,128]{2,1,0:T(8,128)}), f32[8,128,128]{2,1,0:T(8,128)S(1)}, u32[]{:S(2)}, u32[]{:S(2)}) async-start(f32[8,128,128]{2,1,0:T(8,128)} %bitcast.16), calls=%async_computation.1 | async-start | bytes 1048576 | tf_op jit(solution)/shard_map/all_to_all | solution.py:368

commit v5 on v4

--- a/solution.py
+++ b/solution.py
@@ -117,8 +117,8 @@
 
     count = BLOCK // SUB
     for q in range(count):
+        sub_block(mat, inv, wrow, q)
         beside(q)
-        sub_block(mat, inv, wrow, q)
         if q + 1 < count:
             join(mat, wrow, q)
     for q in range(count, count + len(stages) - 1):
@@ -247,7 +247,7 @@
     u1, u2, l10, l20, l21, inv1, inv2, y0, y1, y2, s, u0, inv0, f0, f1, f2, r, inv, wrow, sems = rest
     kept = (u1, u2, l10, l20, l21, inv1, inv2, y0, y1, y2, s, u0, inv0)
     copies = [pltpu.make_async_copy(store.at[pl.ds(i * members, members), :], kept[i], sems.at[i]) for i in range(PARTS)]
-    for i in (10, 11, 0, 1, 12, 2, 3, 7, 5, 4, 8, 6, 9):
+    for i in (10, 11, 0, 1):
         copies[i].start()
 
     def need(c, *parts):
@@ -256,6 +256,8 @@
 
     state_mean = jnp.mean(state[...], axis=0, keepdims=True)
     need(0, 10)
+    for i in (12, 2, 3, 7, 5, 4, 8, 6, 9):
+        copies[i].start()
 
     def gram(c):
         need(c, 11, 0, 1)

time: 81.7 us -> 81.4 us (level)
  transfers between devices with their start and end apart: 4 -> 4, of which waited for: 2 -> 2; matrix products, arithmetic and copies ran while one was open for 3% -> 4% of each run, Pallas kernels for 26% -> 26%
where the time goes in v5:
time: 81.4 us; the launch traced here: 80.9 us
  Pallas kernels  33 us (41%)
  starting transfers between devices  28.9 us (36%)
  waiting for transfers between devices  12.5 us (15%)
  local copies, waits for them, and re-layouts  4.7 us (6%)
  between operations  0.93 us (1%)
  other arithmetic  0.88 us (1%)
    pallas_call x3, Pallas kernels, call(): pl.pallas_call(lambda *refs: kernel(members, *refs), out_shape=tuple((jax...  33 us
    all_to_all x1, starting transfers between devices, local(): lax.all_to_all(obs_ens, 'grp', split_axis=1, concat_axis=0, tiled=True)  12.9 us
    all_to_all x1, starting transfers between devices, local(): lax.all_to_all(turned, 'grp', split_axis=0, concat_axis=0, tiled=True)  10.2 us
    all_to_all x1, waiting for transfers between devices, local(): lax.all_to_all(obs_ens, 'grp', split_axis=1, concat_axis=0, tiled=True)  8.85 us
    ppermute x2, starting transfers between devices, ring(): lax.ppermute(x, ('mem', 'grp'), [(i, (i + step) % count) for i in range(c...  5.83 us
    unnamed x4, local copies, waits for them, and re-layouts  3.88 us
    ppermute x2, waiting for transfers between devices, ring(): lax.ppermute(x, ('mem', 'grp'), [(i, (i + step) % count) for i in range(c...  3.63 us
  transfers between devices with their start and end apart: 4, of which 2 were waited for; matrix products, arithmetic and copies ran while one was open for 4% of the time, Pallas kernels for 26%

profile of v5, /device:TPU:8, one launch (start us, length us, event | category | flops | bytes accessed | tf_op | source)
XLA Modules:
  0.0 80.9 jit_solution(12044009190838953770)
XLA Ops:
  0.0 1.9 %copy.14 = f32[128,8,128]{2,0,1:T(8,128)} copy(f32[128,8,128]{2,1,0:T(8,128)} %param.8) | data formatting | bytes 1048576 | tf_op args[1]
  1.9 12.9 %all-to-all-start = ((f32[128,8,128]{2,0,1:T(8,128)}), f32[128,8,128]{2,0,1:T(8,128)S(1)}, u32[]{:S(2)}, u32[]{:S(2)}) async-start(f32[128,8,128]{2,0,1:T(8,128)} %copy.14), calls=%async_computation | async-start | bytes 1048576 | tf_op jit(solution)/shard_map/all_to_all | solution.py:364
  15.4 1.9 %copy.18 = f32[128,8,128]{2,0,1:T(8,128)} copy(f32[128,8,128]{2,1,0:T(8,128)} %param.7) | data formatting | bytes 1048576 | tf_op args[0]
  17.4 0.7 reduce
  18.1 8.8 %all-to-all-done = f32[128,8,128]{2,0,1:T(8,128)S(1)} async-done(((f32[128,8,128]{2,0,1:T(8,128)}), f32[128,8,128]{2,0,1:T(8,128)S(1)}, u32[]{:S(2)}, u32[]{:S(2)}) %all-to-all-start) | async-done | bytes 524320 | tf_op jit(solution)/shard_map/all_to_all | solution.py:364
  27.0 0.8 concatenate.3.refs_0_
  27.8 3.0 %collective-permute-start.1 = (f32[1032,128]{1,0:T(8,128)S(1)}, f32[1032,128]{1,0:T(8,128)S(1)}, u32[]{:S(2)}, u32[]{:S(2)}) collective-permute-start(f32[1032,128]{1,0:T(8,128)S(1)} %concatenate.3.refs_0_), channel_id=1, source_target_pairs={{0,767},{1,0},{2,1},{3,2},{4,3},{5,4},{6,5},{7,6},{8,7},{9,8},{10,... | collective-permute-start | bytes 1585160 | tf_op jit(solution)/shard_map/ppermute | solution.py:355
  30.8 2.8 %collective-permute-start = (f32[1032,128]{1,0:T(8,128)S(1)}, f32[1032,128]{1,0:T(8,128)S(1)}, u32[]{:S(2)}, u32[]{:S(2)}) collective-permute-start(f32[1032,128]{1,0:T(8,128)S(1)} %concatenate.3.refs_0_), channel_id=1, source_target_pairs={{0,1},{1,2},{2,3},{3,4},{4,5},{5,6},{6,7},{7,8},{8,9},{9,10},{10,1... | collective-permute-start | bytes 1585160 | tf_op jit(solution)/shard_map/ppermute | solution.py:355
  33.6 0.2 compare_reduce_fusion
  33.8 0.0 copy-start
  33.8 5.5 %shard_map.73 = (f32[1024,128]{1,0:T(8,128)S(1)}, f32[8,128]{1,0:T(8,128)S(1)}, f32[1024,128]{1,0:T(8,128)S(1)}) custom-call(f32[1032,128]{1,0:T(8,128)S(1)} %concatenate.3.refs_0_, s32[1,128]{1,0:T(1,128)S(1)} %slice.18.refs_1_), custom_call_target="tpu_custom_call" | custom-call | flops 4000000000 | bytes 2000000 | tf_op jit(solution)/shard_map/pallas_call | solution.py:318
  39.4 10.2 %all-to-all-start.1 = ((f32[8,128,128]{2,1,0:T(8,128)}), f32[8,128,128]{2,1,0:T(8,128)S(1)}, u32[]{:S(2)}, u32[]{:S(2)}) async-start(f32[8,128,128]{2,1,0:T(8,128)} %bitcast.16), calls=%async_computation.1 | async-start | bytes 1048576 | tf_op jit(solution)/shard_map/all_to_all | solution.py:370
  49.6 0.0 collective-permute-done.1.refs_4_
  49.6 3.6 %collective-permute-done.refs_3_ = f32[1032,128]{1,0:T(8,128)S(1)} collective-permute-done((f32[1032,128]{1,0:T(8,128)S(1)}, f32[1032,128]{1,0:T(8,128)S(1)}, u32[]{:S(2)}, u32[]{:S(2)}) %collective-permute-start) | collective-permute-done | bytes 528416 | tf_op jit(solution)/shard_map/ppermute | solution.py:355
  53.2 15.8 %shard_map.74.refs_2_ = f32[51200,128]{1,0:T(8,128)} custom-call(f32[1024,128]{1,0:T(8,128)S(1)} %get-tuple-element.16.refs_0_, f32[8,128]{1,0:T(8,128)S(1)} %get-tuple-element.17.refs_1_, f32[1024,128]{1,0:T(8,128)S(1)} %get-tuple-element.18.refs_2_, f32[1032,128]{1,0:T(8,128)S(1)} %collective-permute-done.refs_3_, ...), custom_call_target="tpu_custom_call" | custom-call | flops 10000000000 | bytes 2000000 | tf_op jit(solution)/shard_map/pallas_call | solution.py:318
  69.0 0.0 all-to-all-done.1
  69.0 0.0 copy-done
  69.0 11.7 %shard_map.75 = f32[1024,128]{1,0:T(8,128)} custom-call(f32[1024,128]{1,0:T(8,128)S(1)} %bitcast.14, s32[1,128]{1,0:T(1,128)S(1)} %copy-done, f32[51200,128]{1,0:T(8,128)} %shard_map.74.refs_2_), custom_call_target="tpu_custom_call" | custom-call | flops 8000000000 | bytes 2000000 | tf_op jit(solution)/shard_map/pallas_call | solution.py:318
  (8 shorter events, 0.0 us)
Async XLA Ops:
  1.9 25.0 %all-to-all-start = ((f32[128,8,128]{2,0,1:T(8,128)}), f32[128,8,128]{2,0,1:T(8,128)S(1)}, u32[]{:S(2)}, u32[]{:S(2)}) async-start(f32[128,8,128]{2,0,1:T(8,128)} %copy.14), calls=%async_computation | async-start | bytes 1048576 | tf_op jit(solution)/shard_map/all_to_all | solution.py:364
  27.8 21.8 %collective-permute-start.1 = (f32[1032,128]{1,0:T(8,128)S(1)}, f32[1032,128]{1,0:T(8,128)S(1)}, u32[]{:S(2)}, u32[]{:S(2)}) collective-permute-start(f32[1032,128]{1,0:T(8,128)S(1)} %concatenate.3.refs_0_), channel_id=1, source_target_pairs={{0,767},{1,0},{2,1},{3,2},{4,3},{5,4},{6,5},{7,6},{8,7},{9,8},{10,... | collective-permute-start | bytes 1585160 | tf_op jit(solution)/shard_map/ppermute | solution.py:355
  30.8 22.4 %collective-permute-start = (f32[1032,128]{1,0:T(8,128)S(1)}, f32[1032,128]{1,0:T(8,128)S(1)}, u32[]{:S(2)}, u32[]{:S(2)}) collective-permute-start(f32[1032,128]{1,0:T(8,128)S(1)} %concatenate.3.refs_0_), channel_id=1, source_target_pairs={{0,1},{1,2},{2,3},{3,4},{4,5},{5,6},{6,7},{7,8},{8,9},{9,10},{10,1... | collective-permute-start | bytes 1585160 | tf_op jit(solution)/shard_map/ppermute | solution.py:355
  33.8 35.2 %copy-start = (s32[1,128]{1,0:T(1,128)S(1)}, s32[1,128]{1,0:T(1,128)}, u32[]{:S(2)}) copy-start(s32[1,128]{1,0:T(1,128)} %refs_1_.1) | copy-start | bytes 1540
  39.4 29.6 %all-to-all-start.1 = ((f32[8,128,128]{2,1,0:T(8,128)}), f32[8,128,128]{2,1,0:T(8,128)S(1)}, u32[]{:S(2)}, u32[]{:S(2)}) async-start(f32[8,128,128]{2,1,0:T(8,128)} %bitcast.16), calls=%async_computation.1 | async-start | bytes 1048576 | tf_op jit(solution)/shard_map/all_to_all | solution.py:370
